TPU v7x, 128 devices: a whole 4x4x4 slice. The times are simulated.
128 devices in a mesh: side: 2 (over core), dev: 64 (over x, y, z).
Axes of the slice: x: 4, y: 4, z: 4, core: 2. Of those that a mesh axis runs over, the one named last changes fastest.
Arguments:
- queries: bfloat16 [1024, 64, 576], P(('side', 'dev')), may hold values from -6 to 6
- latent_cache: bfloat16 [1024, 1024, 576], P(('side', 'dev')), may hold values from -6 to 6
- cache_lengths: int32 [1024], P(('side', 'dev')), may hold values from 256 to 1024, as said below
- residual: bfloat16 [1024, 7168], P('side', 'dev'), may hold values from -6 to 6
- value_up: bfloat16 [64, 512, 128], P('dev'), may hold values from -0.25 to 0.25
- out_proj: bfloat16 [8192, 7168], P(None, 'dev'), may hold values from -0.0625 to 0.0625
- norm_gain: bfloat16 [7168], P('dev'), may hold values from 0.25 to 1.75
- expert_ids: int32 [1024, 8], P('side'), may hold values from 0 to 255, all different within a row; in each aligned block of 512 rows (0 to 511, 512 to 1023, ...) at most 32 rows name the same one
- route_weights: float32 [1024, 8], P('side'), may hold values from 0.3 to 3
- w_gate: bfloat16 [7168, 32768], P(None, ('side', 'dev')), may hold values from -0.0625 to 0.0625
- w_up: bfloat16 [7168, 32768], P(None, ('side', 'dev')), may hold values from -0.0625 to 0.0625
- w_down: bfloat16 [32768, 7168], P(('side', 'dev')), may hold values from -0.1875 to 0.1875
Outputs:
- layer_out: bfloat16 [1024, 7168], P('side', 'dev')
Inputs may be any that keep to these rules, and one draw needn't show every extreme that they name: `expert_ids`: among the 512 requests of one group no expert is named by more than 32 of them, and one expert is named by exactly 32; a row names 8 different experts. `cache_lengths`: request 0 has all 1024 positions valid.
All inputs are finite; a program needn't handle non-finite values.
Results may differ from a plain program's by a relative error of at most 0.007.
Values may be sent and summed in bfloat16 or wider, within the bound.
A program may use at most 128 MiB of HBM per device.

v0:
```python
import jax
import jax.numpy as jnp
from jax import lax
from jax.sharding import PartitionSpec as P

EXPERTS = 256
TOP = 8
SHARDS = 4


score_scale = 192.0 ** (-0.5)
norm_eps = 1e-06


def slot_tables(route_ids, weights_given, experts_window, capacity):
    matches = route_ids[:, :, None] == jnp.arange(experts_window, dtype=jnp.int32)[None, None, :]
    chosen = jnp.any(matches, axis=1).astype(jnp.int32)
    position = jnp.cumsum(chosen, axis=0) - chosen
    slot_hit = (position[:, :, None] == jnp.arange(capacity, dtype=jnp.int32)[None, None, :]) & (
        chosen[:, :, None] > 0
    )
    weight_te = jnp.sum(jnp.where(matches, weights_given[:, :, None], jnp.float32(0.0)), axis=1)
    return (slot_hit, weight_te)


def per_device(
    queries,
    latent_cache,
    cache_lengths,
    residual,
    value_up,
    out_proj,
    norm_gain,
    expert_ids,
    route_weights,
    w_gate,
    w_up,
    w_down,
):
    side_count = lax.axis_size("side")
    dev_count = lax.axis_size("dev")
    latent_width = value_up.shape[1]
    group_rows = expert_ids.shape[0]
    column_count = out_proj.shape[1]
    full_width = column_count * dev_count
    scores = (
        jnp.einsum("rhk,rpk->rhp", queries, latent_cache, preferred_element_type=jnp.float32)
        * score_scale
    )
    valid = jnp.arange(latent_cache.shape[1], dtype=jnp.int32)[None, :] < cache_lengths[:, None]
    scores = jnp.where(valid[:, None, :], scores, jnp.float32(-1e30))
    attn_weights = jax.nn.softmax(scores, axis=-1).astype(jnp.bfloat16)
    contexts = jnp.einsum(
        "rhp,rpl->rhl",
        attn_weights,
        latent_cache[:, :, :latent_width],
        preferred_element_type=jnp.float32,
    ).astype(jnp.bfloat16)
    by_head = lax.all_to_all(contexts, "dev", split_axis=1, concat_axis=0, tiled=True)
    values = jnp.einsum(
        "thl,hlv->thv", by_head, value_up, preferred_element_type=jnp.float32
    ).astype(jnp.bfloat16)
    values = values.reshape(group_rows, value_up.shape[0] * value_up.shape[2])
    attended = jnp.dot(
        lax.all_gather(values, "dev", axis=1, tiled=True),
        out_proj,
        preferred_element_type=jnp.float32,
    )
    hidden = residual.astype(jnp.float32) + attended
    square_sums = lax.psum(jnp.sum(hidden * hidden, axis=1), "dev")
    normed = (
        hidden
        * lax.rsqrt(square_sums[:, None] / full_width + norm_eps)
        * norm_gain.astype(jnp.float32)
    ).astype(jnp.bfloat16)
    experts_window = side_count * dev_count // SHARDS
    capacity = max(2, 2 * group_rows * TOP // EXPERTS)
    slot_hit, weight_te = slot_tables(expert_ids, route_weights, experts_window, capacity)
    outgoing = jnp.einsum(
        "tec,td->ecd", slot_hit.astype(jnp.bfloat16), normed, preferred_element_type=jnp.float32
    ).astype(jnp.bfloat16)
    outgoing = jnp.repeat(outgoing, SHARDS, axis=0)
    arrived = lax.all_to_all(
        outgoing, ("side", "dev"), split_axis=0, concat_axis=0, tiled=True
    ).reshape(side_count, dev_count, capacity, column_count)
    token_rows = arrived.transpose(0, 2, 1, 3).reshape(side_count * capacity, full_width)
    gate_part = jnp.dot(token_rows, w_gate, preferred_element_type=jnp.float32)
    up_part = jnp.dot(token_rows, w_up, preferred_element_type=jnp.float32)
    activated = (jax.nn.silu(gate_part) * up_part).astype(jnp.bfloat16)
    partial_value = jnp.dot(activated, w_down, preferred_element_type=jnp.float32)
    partial_value = partial_value.reshape(side_count, capacity, dev_count, column_count).transpose(
        0, 2, 1, 3
    )
    returned = lax.all_to_all(
        partial_value.reshape(side_count * dev_count, capacity, column_count),
        ("side", "dev"),
        split_axis=0,
        concat_axis=0,
        tiled=True,
    )
    expert_out = jnp.sum(returned.reshape(experts_window, SHARDS, capacity, column_count), axis=1)
    combine = slot_hit.astype(jnp.float32) * weight_te[:, :, None]
    routed = jnp.einsum("tec,ecd->td", combine, expert_out, precision=lax.Precision.HIGHEST)
    return (hidden + routed).astype(jnp.bfloat16)


def solution(mesh):
    placed = (
        P(("side", "dev"), None, None),
        P(("side", "dev"), None, None),
        P(("side", "dev")),
        P("side", "dev"),
        P("dev", None, None),
        P(None, "dev"),
        P("dev"),
        P("side", None),
        P("side", None),
        P(None, ("side", "dev")),
        P(None, ("side", "dev")),
        P(("side", "dev"), None),
    )
    return jax.shard_map(
        per_device, mesh=mesh, in_specs=placed, out_specs=P("side", "dev"), check_vma=False
    )
```

profile of v0, /device:TPU:1, one launch (start us, length us, event | category | flops | bytes accessed | tf_op | source)
XLA Modules:
  0.0 415.2 jit_solution(5061526372324976136)
XLA Ops:
  6.5 0.0 copy-start
  6.5 0.0 all-gather.2.cloned.1.call-start
  6.5 0.9 iota_compare_fusion.2
  7.4 5.8 %fusion.57 = f32[8,64,1024]{2,1,0:T(8,128)S(1)} fusion(bf16[8,64,576]{2,1,0:T(8,128)(2,1)} %param.12, bf16[8,1024,576]{1,2,0:T(8,128)(2,1)} %param.13), kind=kOutput, calls=%fused_computation.64 | convolution fusion | flops 603979776 | bytes 12124160 | tf_op jit(solution)/shard_map/rhk,rpk->rhp/dot_general | solution.py:47
  13.2 0.0 copy-start.1
  13.2 1.3 copy-done.1
  14.5 0.7 fusion.56
  15.2 6.7 %fusion.9 = bf16[8,64,512]{2,1,0:T(8,128)(2,1)S(1)} fusion(bf16[8,1024,576]{1,2,0:T(8,128)(2,1)} %param.13, f32[8,64]{1,0:T(8,128)S(1)} %fusion.56, f32[8,64,1024]{2,1,0:T(8,128)} %copy-done.1, pred[8,1024]{1,0:T(8,128)(4,1)S(1)} %iota_compare_fusion.2), kind=kOutput, calls=%fused_computation.14 | convolution fusion | flops 539756032 | bytes 11020288 | tf_op jit(solution)/shard_map/rhp,rpl->rhl/dot_general | solution.py:53
  22.0 0.0 copy-start.2
  22.0 0.0 copy-start.4
  22.0 0.0 copy-start.6
  22.0 0.0 copy-start.3
  22.0 0.3 copy.45
  22.3 23.4 %all_to_all.25 = bf16[8,64,512]{2,0,1:T(8,128)(2,1)S(1)} all-to-all(bf16[8,64,512]{2,0,1:T(8,128)(2,1)S(1)} %copy.45), channel_id=1, replica_groups=mesh['side'=2,'dev'=64] {'dev'}, dimensions={1} | all-to-all | bytes 1048576 | tf_op jit(solution)/shard_map/all_to_all | solution.py:59
  45.7 0.0 copy-done.2
  45.7 1.0 convolution_convert_fusion
  46.7 0.0 all-gather.2.cloned.1.call-update
  46.7 0.0 copy-done.4
  46.7 0.1 fusion.34
  46.8 1.2 reduce-window.6
  48.0 0.2 slice_reduce_fusion
  48.3 0.0 copy-done.6
  48.3 0.1 convert_subtract_fusion
  48.4 0.3 fusion.5
  48.7 93.3 %all-gather.2.cloned.1.call-done = bf16[512,8192]{1,0:T(8,128)(2,1)} async-done(((bf16[512,128]{1,0:T(8,128)(2,1)}), bf16[512,8192]{1,0:T(8,128)(2,1)}) %all-gather.2.cloned.1.call-update) | async-done | bytes 8388624 | tf_op jit(solution)/shard_map/all_gather | solution.py:65
  142.0 0.0 copy-done
  142.0 0.0 copy-done.3
  142.0 6.2 %multiply_reduce_fusion = (f32[512]{0:T(512)S(1)}, f32[512,112]{0,1:T(8,128)S(1)}) fusion(bf16[512,8192]{1,0:T(8,128)(2,1)} %all-gather.2.cloned.1.call-done, bf16[8192,112]{0,1:T(8,128)(2,1)S(1)} %copy-done, bf16[512,112]{0,1:T(8,128)(2,1)S(1)} %copy-done.3), kind=kOutput, calls=%fused_computation.36 | convolution fusion | flops 939752960 | bytes 10569728 | tf_op jit(solution)/shard_map/dot_general | solution.py:64
  148.3 149.2 %psum.7 = f32[512]{0:T(512)S(1)} all-reduce(f32[512]{0:T(512)S(1)} %get-tuple-element.7), channel_id=1, replica_groups=mesh['side'=2,'dev'=64] {'dev'}, use_global_device_ids=true, to_apply=%region_7.8 | all-reduce | flops 512 | bytes 4096 | tf_op jit(solution)/shard_map/psum | solution.py:70
  297.5 1.1 fusion.12
  298.6 0.2 broadcast_in_dim.30
  298.7 49.6 %all_to_all.26 = bf16[128,32,112]{2,1,0:T(8,128)(2,1)S(1)} all-to-all(bf16[128,32,112]{2,1,0:T(8,128)(2,1)S(1)} %bitcast.57), channel_id=1, replica_groups=mesh['side'=2,'dev'=64] {'side','dev'}, dimensions={0} | all-to-all | bytes 1835008 | tf_op jit(solution)/shard_map/all_to_all | solution.py:83
  348.3 1.4 copy.49
  349.7 2.7 reshape.78
  352.4 2.8 fusion.58
  355.2 6.7 %fusion.25 = f32[64,7168]{1,0:T(8,128)} fusion(bf16[256,7168]{1,0:T(8,128)(2,1)} %param.23, bf16[64,7168]{1,0:T(8,128)(2,1)S(1)} %reshape.78, bf16[7168,256]{1,0:T(8,128)(2,1)} %param.22, f32[64,256]{1,0:T(8,128)S(1)} %fusion.58), kind=kOutput, calls=%fused_computation.23 | convolution fusion | flops 469860352 | bytes 10158080 | tf_op jit(solution)/shard_map/dot_general | solution.py:90
  361.9 3.4 reshape.79
  365.3 4.1 copy.50
  369.4 0.0 copy-start.5
  369.4 6.1 %all-to-all-start.2 = ((f32[128,32,112]{2,1,0:T(8,128)}), f32[128,32,112]{2,1,0:T(8,128)}, u32[]{:S(2)}, u32[]{:S(2)}) async-start(f32[128,32,112]{2,1,0:T(8,128)} %bitcast.56), calls=%async_computation.2 | async-start | bytes 4194304 | tf_op jit(solution)/shard_map/all_to_all | solution.py:94
  375.5 0.0 copy-done.5
  375.5 0.1 select_reduce_fusion
  375.5 28.3 %all-to-all-done.2 = f32[128,32,112]{2,1,0:T(8,128)} async-done(((f32[128,32,112]{2,1,0:T(8,128)}), f32[128,32,112]{2,1,0:T(8,128)}, u32[]{:S(2)}, u32[]{:S(2)}) %all-to-all-start.2) | async-done | bytes 1835040 | tf_op jit(solution)/shard_map/all_to_all | solution.py:94
  403.9 1.9 bitcast_reduce_fusion
  405.8 2.6 fusion.21
  (6 shorter events, 0.1 us)
Async XLA Ops:
  6.5 135.5 %copy-start = (bf16[8192,112]{0,1:T(8,128)(2,1)S(1)}, bf16[8192,112]{0,1:T(8,128)(2,1)}, u32[]{:S(2)}) copy-start(bf16[8192,112]{0,1:T(8,128)(2,1)} %param.17) | copy-start | bytes 5505028
  6.5 135.5 %all-gather.2.cloned.1.call-start = ((), (), s32[]{:S(2)}) async-start(), calls=%async_computation.3 | async-start | bytes 8519680 | tf_op jit(solution)/shard_map/all_gather | solution.py:65
  13.2 1.4 copy-start.1
  22.0 23.8 %copy-start.2 = (bf16[1,512,128]{2,1,0:T(8,128)(2,1)S(1)}, bf16[1,512,128]{2,1,0:T(8,128)(2,1)}, u32[]{:S(2)}) copy-start(bf16[1,512,128]{2,1,0:T(8,128)(2,1)} %param.16) | copy-start | bytes 393220
  22.0 24.7 %copy-start.4 = (s32[512,8]{0,1:T(8,128)S(1)}, s32[512,8]{0,1:T(8,128)}, u32[]{:S(2)}) copy-start(s32[512,8]{0,1:T(8,128)} %param.19) | copy-start | bytes 49156
  22.0 26.3 %copy-start.6 = (bf16[112]{0:T(256)(128)(2,1)S(1)}, bf16[112]{0:T(256)(128)(2,1)}, u32[]{:S(2)}) copy-start(bf16[112]{0:T(256)(128)(2,1)} %param.18) | copy-start | bytes 676
  22.0 120.0 %copy-start.3 = (bf16[512,112]{0,1:T(8,128)(2,1)S(1)}, bf16[512,112]{0,1:T(8,128)(2,1)}, u32[]{:S(2)}) copy-start(bf16[512,112]{0,1:T(8,128)(2,1)} %param.15) | copy-start | bytes 344068
  369.4 6.1 %copy-start.5 = (f32[512,8]{0,1:T(8,128)S(1)}, f32[512,8]{0,1:T(8,128)}, u32[]{:S(2)}) copy-start(f32[512,8]{0,1:T(8,128)} %param.20) | copy-start | bytes 49156
  369.4 34.5 %all-to-all-start.2 = ((f32[128,32,112]{2,1,0:T(8,128)}), f32[128,32,112]{2,1,0:T(8,128)}, u32[]{:S(2)}, u32[]{:S(2)}) async-start(f32[128,32,112]{2,1,0:T(8,128)} %bitcast.56), calls=%async_computation.2 | async-start | bytes 4194304 | tf_op jit(solution)/shard_map/all_to_all | solution.py:94
Sparse Core Ops, SparseCore 0:
  46.8 95.1 all-gather.1
where the time goes:
time: 416 us; the launch traced here: 415 us
  blocking collectives  222 us (53%)
  waiting for transfers between devices  122 us (29%)
  matrix products  32.8 us (8%)
  local copies, waits for them, and re-layouts  13.7 us (3%)
  between operations  13.6 us (3%)
  starting transfers between devices  6.08 us (1%)
  other arithmetic  5.26 us (1%)
    psum x1, blocking collectives, per_device(): square_sums = lax.psum(jnp.sum(hidden * hidden, axis=1), 'dev')  149 us
    all_gather x1, waiting for transfers between devices, per_device(): lax.all_gather(values, 'dev', axis=1, tiled=True)  93.3 us
    all_to_all x1, blocking collectives, per_device(): lax.all_to_all(outgoing, ('side', 'dev'), split_axis=0, concat_axis=0, ti...  49.6 us
    all_to_all x1, waiting for transfers between devices, per_device(): lax.all_to_all(partial_value.reshape(side_count * dev_count, capacity, co...  28.3 us
    all_to_all x1, blocking collectives, per_device(): lax.all_to_all(contexts, 'dev', split_axis=1, concat_axis=0, tiled=True)  23.4 us
  transfers between devices with their start and end apart: 2, of which 2 were waited for; matrix products, arithmetic and copies ran while one was open for 0% of the time, Pallas kernels for 0%

commit v1 on v0

v1 whole, which is shorter than its diff:
```python
import functools

import jax
import jax.numpy as jnp
from jax import lax
from jax.experimental import pallas as pl
from jax.experimental.pallas import tpu as pltpu
from jax.sharding import PartitionSpec as P

MESH = pl.DeviceIdType.MESH
LANES = 128
SCORE_SCALE = 192.0 ** (-0.5)
NORM_EPS = 1e-06
BF16 = jnp.bfloat16
F32 = jnp.float32


def nt_dot(a, b):
    return lax.dot_general(a, b, (((1,), (1,)), ((), ())), preferred_element_type=F32)


def nn_dot(a, b):
    return jnp.dot(a, b, preferred_element_type=F32)


def layer_kernel(
    dims,
    q_ref,
    cache_ref,
    len_ref,
    res_ref,
    vu_ref,
    wo_ref,
    gain_ref,
    ids_ref,
    rw_ref,
    wg_ref,
    wu_ref,
    wd_ref,
    out_ref,
    cache_v,
    wg_v,
    wu_v,
    wd_v,
    wo_v,
    vu_v,
    ctx_f,
    ctx_send,
    ctx_recv,
    val_v,
    part_send,
    part_recv,
    part_own,
    res_v,
    hid_v,
    hid_t,
    pos_v,
    wte_v,
    onehot,
    wslot,
    disp,
    rows,
    osend,
    ret,
    cache_sem,
    weight_sem,
    wo_sem,
    wo_send_sem,
    wo_recv_sem,
    vu_sem,
    vu_send_sem,
    vu1_sem,
    vu2_sem,
    sib_send_sem,
    sib_recv_sem,
    ctx_send_sem,
    ctx_recv_sem,
    ag_send_sem,
    ag1_sem,
    ag2_sem,
    rs_send_sem,
    rs_recv_sem,
    disp_send_sem,
    disp_recv_sem,
    ret_send_sem,
    ret_recv_sem,
):
    side_n, nx, nz = dims["side"], dims["x"], dims["z"]
    ny = nx
    plane = nx * ny
    ndev = plane * nz
    reqs, heads, _ = q_ref.shape
    length = cache_ref.shape[2]
    latent = vu_ref.shape[1]
    vdim = vu_ref.shape[2]
    cols = res_ref.shape[0]
    tokens = res_ref.shape[1]
    blk = nz * reqs
    chunk = ny * blk
    half = plane // side_n
    experts = side_n * plane
    cap = onehot.shape[0] // experts
    full = ndev * cols
    side = lax.axis_index("side")
    dev = lax.axis_index("dev")
    x = dev // (ny * nz)
    y = (dev // nz) % ny
    z = dev % nz
    own_block = x * ny + y
    up = jnp.where(side == 0, x, y)
    uq = jnp.where(side == 0, y, x)
    twin = 1 - side

    def block_of(w, u):
        return jnp.where(side == 0, w * ny + u, u * ny + w)

    def at_plane(block):
        return {"side": side, "dev": block * nz + z}

    def at_ring(zz):
        return {"side": side, "dev": own_block * nz + zz}

    def remote(src, dst, send, recv, target):
        return pltpu.make_async_remote_copy(
            src_ref=src, dst_ref=dst, send_sem=send, recv_sem=recv, device_id=target, device_id_type=MESH
        )

    def drain(ref, sem):
        pltpu.make_async_copy(ref, ref, sem).wait()

    def rows_at(start, size):
        return pl.ds(pl.multiple_of(start, size), size)

    for r in range(reqs):
        pltpu.make_async_copy(cache_ref.at[r], cache_v.at[r], cache_sem.at[r]).start()
    half_lanes = half * LANES
    half_rows = latent // side_n
    my_half = pl.ds(pl.multiple_of(side * half_lanes, half_lanes), half_lanes)
    my_rows = rows_at(side * half_rows, half_rows)

    def wo_source(j, zz):
        return wo_ref.at[:, rows_at((j * nz + zz) * LANES, LANES)]

    def wo_place(zz, j):
        return wo_v.at[zz, pl.ds(0, cols), rows_at(j * LANES, LANES)]

    for zz in range(nz):
        wo_v[zz, cols:, :] = jnp.zeros((LANES - cols, plane * LANES), BF16)
    for i in range(half):
        j = side * half + i
        pltpu.make_async_copy(wo_source(j, z), wo_place(z, j), wo_sem).start()
    own_vu = pltpu.make_async_copy(vu_ref.at[0, my_rows, :], vu_v.at[own_block, my_rows, :], vu_sem)
    own_vu.start()
    pltpu.make_async_copy(wg_ref, wg_v.at[:, pl.ds(0, cols), :], weight_sem.at[0]).start()
    pltpu.make_async_copy(wu_ref, wu_v.at[:, pl.ds(0, cols), :], weight_sem.at[1]).start()
    pltpu.make_async_copy(wd_ref, wd_v, weight_sem.at[2]).start()

    barrier = pltpu.get_barrier_semaphore()

    def greet(i, carry):
        other = lax.rem(side * ndev + dev + i, side_n * ndev)
        pl.semaphore_signal(
            barrier, inc=1, device_id={"side": other // ndev, "dev": other % ndev}, device_id_type=MESH
        )
        return carry

    lax.fori_loop(1, side_n * ndev, greet, 0)

    def attend(r):
        pltpu.make_async_copy(cache_ref.at[r], cache_v.at[r], cache_sem.at[r]).wait()
        scores = nn_dot(q_ref[r], cache_v[r]) * SCORE_SCALE
        valid = lax.broadcasted_iota(jnp.int32, scores.shape, 1) < len_ref[r]
        scores = jnp.where(valid, scores, -1e30)
        weights = jnp.exp(scores - jnp.max(scores, axis=1, keepdims=True))
        weights = (weights / jnp.sum(weights, axis=1, keepdims=True)).astype(BF16)
        context = nt_dot(weights, cache_v[r, 0:latent, :])
        for b in range(latent // LANES):
            ctx_f[b, r * heads : (r + 1) * heads, :] = context[:, b * LANES : (b + 1) * LANES]

    quarter = reqs // 4
    for r in range(quarter):
        attend(r)

    pl.semaphore_wait(barrier, side_n * ndev - 1)
    for k in range(1, nx):
        remote(
            vu_ref.at[0, my_rows, :],
            vu_v.at[own_block, my_rows, :],
            vu_send_sem,
            vu1_sem.at[k - 1],
            at_plane(block_of(up, (uq + k) % ny)),
        ).start()
    for k in range(1, nz):
        to = (z + k) % nz
        for i in range(half):
            j = side * half + i
            remote(wo_source(j, to), wo_place(z, j), wo_send_sem, wo_recv_sem.at[k - 1], at_ring(to)).start()
    own_vu.wait()

    def forward_vu(a):
        block = block_of(up, (uq + ny - a) % ny)
        piece = vu_v.at[block, my_rows, :]
        if a > 0:
            pltpu.make_async_copy(piece, piece, vu1_sem.at[a - 1]).wait()
        for k in range(1, nx):
            to = at_plane(block_of((up + k) % nx, uq))
            remote(piece, piece, vu_send_sem, vu2_sem.at[k - 1, a], to).start()

    forward_vu(0)
    for r in range(quarter, 2 * quarter):
        attend(r)
    for a in range(1, ny):
        forward_vu(a)
    for r in range(2 * quarter, reqs):
        attend(r)

    def pack(jp, zz):
        parts = []
        for j in (2 * jp, 2 * jp + 1):
            pieces = [
                ctx_f[b, pl.ds(j * nz + zz, reqs, stride=heads), :] for b in range(latent // LANES)
            ]
            parts.append(jnp.concatenate(pieces, axis=1))
        return jnp.concatenate(parts, axis=0).astype(BF16)

    for zz in range(nz):
        for jp in range(plane // 2):
            ctx_send[zz, jp * 2 * reqs : (jp + 1) * 2 * reqs, :] = pack(jp, zz)
    for k in range(1, nz):
        to = (z + k) % nz
        remote(ctx_send.at[to], ctx_recv.at[z], ctx_send_sem, ctx_recv_sem.at[k - 1], at_ring(to)).start()
    ctx_recv[z] = ctx_send[z]

    for k in range(1, nx):
        for a in range(ny):
            piece = vu_v.at[block_of((up + nx - k) % nx, (uq + ny - a) % ny), my_rows, :]
            pltpu.make_async_copy(piece, piece, vu2_sem.at[k - 1, a]).wait()
    mate = {"side": twin, "dev": dev}
    vu_half = vu_v.at[:, my_rows, :]
    vu_swap = remote(vu_half, vu_half, sib_send_sem.at[0], sib_recv_sem.at[0], mate)
    vu_swap.start()
    wo_half = wo_v.at[:, :, my_half]
    own_wo = wo_v.at[z, pl.ds(0, cols), my_half]
    pltpu.make_async_copy(own_wo, own_wo, wo_sem).wait()
    for k in range(1, nz):
        piece = wo_v.at[(z + nz - k) % nz, pl.ds(0, cols), my_half]
        pltpu.make_async_copy(piece, piece, wo_recv_sem.at[k - 1]).wait()
    wo_swap = remote(wo_half, wo_half, sib_send_sem.at[1], sib_recv_sem.at[1], mate)
    wo_swap.start()

    ids = ids_ref[...]
    rw = rw_ref[...]
    expert_no = lax.broadcasted_iota(jnp.int32, (experts, tokens), 0)
    chosen = jnp.zeros((experts, tokens), F32)
    wte = jnp.zeros((experts, tokens), F32)
    for k in range(ids.shape[0]):
        match = ids[k : k + 1, :] == expert_no
        chosen = jnp.where(match, 1.0, chosen)
        wte = wte + jnp.where(match, rw[k : k + 1, :], 0.0)
    before = lax.broadcasted_iota(jnp.int32, (tokens, tokens), 0) < lax.broadcasted_iota(
        jnp.int32, (tokens, tokens), 1
    )
    position = nn_dot(chosen.astype(BF16), jnp.where(before, 1.0, 0.0).astype(BF16))
    pos_v[...] = jnp.where(chosen > 0.0, position, -1.0)
    wte_v[...] = wte

    def fill(e, carry):
        slot = lax.broadcasted_iota(jnp.int32, (cap, tokens), 0).astype(F32)
        hit = pos_v[pl.ds(e, 1), :] == slot
        onehot[rows_at(e * cap, cap), :] = jnp.where(hit, 1.0, 0.0).astype(BF16)
        picked = jnp.sum(jnp.where(hit, wte_v[pl.ds(e, 1), :], 0.0), axis=1, keepdims=True)
        wslot[rows_at(e * cap, cap), :] = jnp.broadcast_to(picked, (cap, LANES))
        return carry

    lax.fori_loop(0, experts, fill, 0)
    res_t = jnp.concatenate(
        [res_ref[...].astype(F32), jnp.zeros((LANES - cols, tokens), F32)], axis=0
    )
    res_v[...] = res_t.T
    for d in range(ndev):
        wg_v[d, cols:, :] = jnp.zeros((LANES - cols, wg_v.shape[2]), BF16)
        wu_v[d, cols:, :] = jnp.zeros((LANES - cols, wu_v.shape[2]), BF16)
    part_recv[z] = jnp.zeros((tokens, LANES), BF16)

    vu_swap.wait_recv()
    for k in range(1, nz):
        piece = ctx_recv.at[(z + nz - k) % nz]
        pltpu.make_async_copy(piece, piece, ctx_recv_sem.at[k - 1]).wait()
    my_block = rows_at(own_block * blk, blk)
    two = 2 * reqs
    for jp in range(plane // 2):
        lhs = jnp.concatenate([ctx_recv[zz, jp * two : (jp + 1) * two, :] for zz in range(nz)], axis=0)
        rhs = jnp.concatenate([vu_v[2 * jp], vu_v[2 * jp + 1]], axis=1)
        both = nn_dot(lhs, rhs)
        picked = [
            jnp.concatenate(
                [
                    both[zz * two : zz * two + reqs, 0:vdim],
                    both[zz * two + reqs : (zz + 1) * two, vdim : 2 * vdim],
                ],
                axis=1,
            )
            for zz in range(nz)
        ]
        val_v[my_block, jp * 2 * vdim : (jp + 1) * 2 * vdim] = jnp.concatenate(picked, axis=0).astype(BF16)

    mine = val_v.at[my_block, :]
    for k in range(1, ny):
        remote(mine, mine, ag_send_sem, ag1_sem.at[k - 1], at_plane(block_of(up, (uq + k) % ny))).start()
    for a in range(ny):
        piece = val_v.at[rows_at(block_of(up, (uq + ny - a) % ny) * blk, blk), :]
        if a > 0:
            pltpu.make_async_copy(piece, piece, ag1_sem.at[a - 1]).wait()
        for k in range(1, nx):
            to = at_plane(block_of((up + k) % nx, uq))
            remote(piece, piece, ag_send_sem, ag2_sem.at[k - 1, a], to).start()
    wo_swap.wait_recv()
    for k in range(nx):
        w = (up + nx - k) % nx
        if k > 0:
            for a in range(ny):
                piece = val_v.at[rows_at(block_of(w, (uq + ny - a) % ny) * blk, blk), :]
                pltpu.make_async_copy(piece, piece, ag2_sem.at[k - 1, a]).wait()
        lhs = jnp.concatenate([val_v[rows_at(block_of(w, u) * blk, blk), :] for u in range(ny)], axis=0)
        at = rows_at(w * chunk, chunk)
        own = jnp.zeros((chunk, LANES), F32)
        for zz in range(nz):
            part = nt_dot(lhs, wo_v[zz])
            own = jnp.where(z == zz, part, own)
            part_send[zz, at, :] = part.astype(BF16)
        part_own[at, :] = own
        for kk in range(1, nz):
            to = (z + kk) % nz
            remote(
                part_send.at[to, at, :], part_recv.at[z, at, :], rs_send_sem, rs_recv_sem.at[kk - 1, k], at_ring(to)
            ).start()
    for k in range(nx):
        at = rows_at(((up + nx - k) % nx) * chunk, chunk)
        for kk in range(1, nz):
            piece = part_recv.at[(z + nz - kk) % nz, at, :]
            pltpu.make_async_copy(piece, piece, rs_recv_sem.at[kk - 1, k]).wait()
    for w in range(nx):
        for u in range(ny):
            here = (w * ny + u) * blk
            total = part_own[here : here + blk, :]
            for zz in range(nz):
                total = total + part_recv[zz, here : here + blk, :].astype(F32)
            there = rows_at(block_of(w, u) * blk, blk)
            hid_v[there, :] = total + res_v[there, :]

    hidden = hid_v[...]
    squares = jnp.sum(hidden * hidden, axis=1, keepdims=True)
    high = squares.astype(BF16).astype(F32)
    middle = (squares - high).astype(BF16).astype(F32)
    low = squares - high - middle
    lane = lax.broadcasted_iota(jnp.int32, (tokens, LANES), 1)
    gain = jnp.concatenate([gain_ref[...].astype(F32), jnp.zeros((1, LANES - cols), F32)], axis=1)
    extended = hidden * gain
    extended = jnp.where(lane == cols, high, extended)
    extended = jnp.where(lane == cols + 1, middle, extended)
    extended = jnp.where(lane == cols + 2, low, extended)
    disp[...] = nn_dot(onehot[...], extended.astype(BF16)).astype(BF16)

    my_lanes = rows_at(dev * LANES, LANES)
    my_slots = rows_at(side * cap, cap)

    def dispatch(i, carry):
        ds = i // ndev
        dd = i % ndev
        sx = (x + dd // (ny * nz)) % nx
        sy = (y + (dd // nz) % ny) % ny
        sz = (z + dd % nz) % nz
        ss = (side + ds) % side_n
        expert = ss * plane + sx * ny + sy
        src = disp.at[rows_at(expert * cap, cap), :]
        remote(
            src,
            rows.at[my_slots, my_lanes],
            disp_send_sem,
            disp_recv_sem.at[x],
            {"side": ss, "dev": (sx * ny + sy) * nz + sz},
        ).start()
        return carry

    own_expert = side * plane + own_block
    pltpu.make_async_copy(
        disp.at[rows_at(own_expert * cap, cap), :], rows.at[my_slots, my_lanes], disp_recv_sem.at[x]
    ).start()
    lax.fori_loop(1, side_n * ndev, dispatch, 0)
    hid_t[...] = hidden.T
    pltpu.make_async_copy(wg_ref, wg_v.at[:, pl.ds(0, cols), :], weight_sem.at[0]).wait()
    pltpu.make_async_copy(wu_ref, wu_v.at[:, pl.ds(0, cols), :], weight_sem.at[1]).wait()
    pltpu.make_async_copy(wd_ref, wd_v, weight_sem.at[2]).wait()

    units = wg_v.shape[2]
    group = ny * nz
    slots = side_n * cap
    gate = jnp.zeros((slots, units), F32)
    upward = jnp.zeros((slots, units), F32)
    marks = jnp.zeros((slots, LANES), F32)
    for k in range(nx):
        sx = (x + nx - k) % nx
        piece = rows.at[:, pl.ds(pl.multiple_of(sx * group * LANES, group * LANES), group * LANES)]
        pltpu.make_async_copy(piece, piece, disp_recv_sem.at[sx]).wait()
        lhs = piece[...]
        gate = gate + nn_dot(lhs, wg_v[pl.ds(sx * group, group)].reshape(group * LANES, units))
        upward = upward + nn_dot(lhs, wu_v[pl.ds(sx * group, group)].reshape(group * LANES, units))
        for d in range(group):
            marks = marks + lhs[:, d * LANES : (d + 1) * LANES].astype(F32)
    mark_lane = lax.broadcasted_iota(jnp.int32, (slots, LANES), 1)
    marks = jnp.where((mark_lane >= cols) & (mark_lane < cols + 3), marks, 0.0)
    scale = lax.rsqrt(jnp.sum(marks, axis=1, keepdims=True) / full + NORM_EPS)
    gate = gate * scale
    activated = (gate / (1.0 + jnp.exp(-gate)) * (upward * scale)).astype(BF16)

    per = 8
    groups = ndev // per
    first = dev // per
    home = rows_at(own_expert * cap, cap)

    def give(i, carry):
        g = (first + i) % groups
        width = per * cols
        out = nn_dot(activated, wd_v[:, pl.ds(pl.multiple_of(g * width, LANES), width)])
        for k in range(per):
            piece = out[:, k * cols : (k + 1) * cols]
            piece = jnp.concatenate([piece, jnp.zeros((slots, LANES - cols), F32)], axis=1)
            osend[:, rows_at((g * per + k) * LANES, LANES)] = piece.astype(BF16)
        for k in range(per):
            for s in range(side_n):
                target = g * per + k
                src = osend.at[s * cap : (s + 1) * cap, rows_at(target * LANES, LANES)]
                here = (side == s) & (dev == target)

                @pl.when(here)
                def _():
                    pltpu.make_async_copy(src, ret.at[z, home, :], ret_recv_sem).start()

                @pl.when(jnp.logical_not(here))
                def _():
                    remote(src, ret.at[z, home, :], ret_send_sem, ret_recv_sem, {"side": s, "dev": target}).start()

        return carry

    lax.fori_loop(0, groups, give, 0)

    drain(ret, ret_recv_sem)
    total = ret[0].astype(F32)
    for zz in range(1, nz):
        total = total + ret[zz].astype(F32)
    total = (total * wslot[...]).T
    high = total.astype(BF16)
    low = (total - high.astype(F32)).astype(BF16)
    routed = nn_dot(jnp.concatenate([high, low], axis=0), onehot[...])
    result = hid_t[...] + routed[0:LANES] + routed[LANES : 2 * LANES]
    out_ref[...] = result[0:cols].astype(BF16)

    drain(wo_v.at[0 : nz - 1, pl.ds(0, cols), my_half], wo_send_sem)
    drain(vu_v.at[0 : (nx - 1) * (ny + 1), my_rows, :], vu_send_sem)
    vu_swap.wait_send()
    wo_swap.wait_send()
    drain(ctx_send.at[0 : nz - 1], ctx_send_sem)
    drain(val_v.at[0 : (nx - 1) * (ny + 1) * blk], ag_send_sem)
    drain(part_send.at[0 : nz - 1], rs_send_sem)
    flat = side_n * ndev - 1
    drain(disp_drain_ref(ret, flat, cap), disp_send_sem)
    drain(disp_drain_ref(ret, flat, cap), ret_send_sem)


def disp_drain_ref(ret, blocks, cap):
    return ret.reshape(ret.shape[0] * ret.shape[1], ret.shape[2]).at[0 : blocks * cap]


def per_device(
    queries,
    latent_cache,
    cache_lengths,
    residual,
    value_up,
    out_proj,
    norm_gain,
    expert_ids,
    route_weights,
    w_gate,
    w_up,
    w_down,
):
    side_n = lax.axis_size("side")
    ndev = lax.axis_size("dev")
    nx = round(ndev ** (1 / 3))
    nz = nx
    plane = nx * nx
    tokens, cols = residual.shape
    reqs, heads, width = queries.shape
    length = latent_cache.shape[1]
    latent, vdim = value_up.shape[1:]
    units = w_gate.shape[1]
    experts = side_n * plane
    cap = 32
    blk = nz * reqs
    vmem = pl.BlockSpec(memory_space=pltpu.VMEM)
    smem = pl.BlockSpec(memory_space=pltpu.SMEM)
    hbm = pl.BlockSpec(memory_space=pl.ANY)
    dma = pltpu.SemaphoreType.DMA
    out = pl.pallas_call(
        functools.partial(layer_kernel, {"side": side_n, "x": nx, "z": nz}),
        out_shape=jax.ShapeDtypeStruct((cols, tokens), BF16),
        in_specs=[vmem, hbm, smem, vmem, hbm, hbm, vmem, vmem, vmem, hbm, hbm, hbm],
        out_specs=vmem,
        scratch_shapes=[
            pltpu.VMEM((reqs, width, length), BF16),
            pltpu.VMEM((ndev, LANES, units), BF16),
            pltpu.VMEM((ndev, LANES, units), BF16),
            pltpu.VMEM((units, ndev * cols), BF16),
            pltpu.VMEM((nz, LANES, plane * LANES), BF16),
            pltpu.VMEM((plane, latent, vdim), BF16),
            pltpu.VMEM((latent // LANES, reqs * heads, LANES), F32),
            pltpu.VMEM((nz, plane * reqs, latent), BF16),
            pltpu.VMEM((nz, plane * reqs, latent), BF16),
            pltpu.VMEM((tokens, plane * LANES), BF16),
            pltpu.VMEM((nz, tokens, LANES), BF16),
            pltpu.VMEM((nz, tokens, LANES), BF16),
            pltpu.VMEM((tokens, LANES), F32),
            pltpu.VMEM((tokens, LANES), F32),
            pltpu.VMEM((tokens, LANES), F32),
            pltpu.VMEM((LANES, tokens), F32),
            pltpu.VMEM((experts, tokens), F32),
            pltpu.VMEM((experts, tokens), F32),
            pltpu.VMEM((experts * cap, tokens), BF16),
            pltpu.VMEM((experts * cap, LANES), F32),
            pltpu.VMEM((experts * cap, LANES), BF16),
            pltpu.VMEM((side_n * cap, ndev * LANES), BF16),
            pltpu.VMEM((side_n * cap, ndev * LANES), BF16),
            pltpu.VMEM((nz, experts * cap, LANES), BF16),
            dma((reqs,)),
            dma((3,)),
            dma(()),
            dma(()),
            dma((nz - 1,)),
            dma(()),
            dma(()),
            dma((nx - 1,)),
            dma((nx - 1, nx)),
            dma((2,)),
            dma((2,)),
            dma(()),
            dma((nz - 1,)),
            dma(()),
            dma((nx - 1,)),
            dma((nx - 1, nx)),
            dma(()),
            dma((nz - 1, nx)),
            dma(()),
            dma((nx,)),
            dma(()),
            dma(()),
        ],
        compiler_params=pltpu.CompilerParams(
            collective_id=0, has_side_effects=True, vmem_limit_bytes=56 * 1024 * 1024
        ),
    )(
        queries,
        latent_cache.transpose(0, 2, 1),
        cache_lengths,
        residual.T,
        value_up,
        out_proj.T,
        norm_gain.reshape(1, cols),
        expert_ids.T,
        route_weights.T,
        w_gate.reshape(ndev, cols, units),
        w_up.reshape(ndev, cols, units),
        w_down,
    )
    return out.T


def solution(mesh):
    placed = (
        P(("side", "dev"), None, None),
        P(("side", "dev"), None, None),
        P(("side", "dev")),
        P("side", "dev"),
        P("dev", None, None),
        P(None, "dev"),
        P("dev"),
        P("side", None),
        P("side", None),
        P(None, ("side", "dev")),
        P(None, ("side", "dev")),
        P(("side", "dev"), None),
    )
    return jax.shard_map(
        per_device, mesh=mesh, in_specs=placed, out_specs=P("side", "dev"), check_vma=False
    )
```

time: 416 us -> 93.7 us (0.23)
  the two profiles are of different devices: /device:TPU:1 before, /device:TPU:25 now
where the time goes in v1:
time: 93.7 us; the launch traced here: 93.6 us
  Pallas kernels  92 us (98%)
  local copies, waits for them, and re-layouts  1.55 us (2%)
    pallas_call x1, Pallas kernels, per_device(): pl.pallas_call(functools.partial(layer_kernel, {'side': side_n, 'x': nx,...  92 us

profile of v1, /device:TPU:25, one launch (start us, length us, event | category | flops | bytes accessed | tf_op | source)
XLA Modules:
  0.0 93.6 jit_solution(17842481142393351953)
XLA Ops:
  0.0 92.0 %shard_map.118 = bf16[112,512]{1,0:T(8,128)(2,1)} custom-call(bf16[8,64,576]{2,1,0:T(8,128)(2,1)} %q_ref.1, bf16[8,576,1024]{2,1,0:T(8,128)(2,1)} %bitcast.9, s32[8]{0:T(128)} %len_ref.1, bf16[112,512]{1,0:T(8,128)(2,1)} %bitcast.14, bf16[1,512,128]{2,1,0:T(8,128)(2,1)} %vu_ref.1, bf16[112,8192]{1,0:T(8,128)(2,1)} %bitcast.12, bf16[1,112]{1,0:T(2,128)(2,1)} %bitcast.17, ...), custom_call_target="tpu_custom_call" | custom-call | tf_op jit(solution)/shard_map/pallas_call | solution.py:505
  92.0 1.6 %copy.14 = bf16[512,112]{0,1:T(8,128)(2,1)} copy(bf16[512,112]{0,1:T(8,128)(2,1)} %bitcast.13) | data formatting | bytes 229376

commit v2 on v1

--- a/solution.py
+++ b/solution.py
@@ -71,8 +71,10 @@
     vu_send_sem,
     vu1_sem,
     vu2_sem,
-    sib_send_sem,
-    sib_recv_sem,
+    vu_swap_send_sem,
+    vu_swap_recv_sem,
+    wo_swap_send_sem,
+    wo_swap_recv_sem,
     ctx_send_sem,
     ctx_recv_sem,
     ag_send_sem,
@@ -156,15 +158,14 @@
     pltpu.make_async_copy(wd_ref, wd_v, weight_sem.at[2]).start()
 
     barrier = pltpu.get_barrier_semaphore()
-
-    def greet(i, carry):
-        other = lax.rem(side * ndev + dev + i, side_n * ndev)
-        pl.semaphore_signal(
-            barrier, inc=1, device_id={"side": other // ndev, "dev": other % ndev}, device_id_type=MESH
-        )
-        return carry
-
-    lax.fori_loop(1, side_n * ndev, greet, 0)
+    mate = {"side": twin, "dev": dev}
+    friends = [mate]
+    for k in range(1, nx):
+        friends.append({"side": side, "dev": (((x + k) % nx) * ny + y) * nz + z})
+        friends.append({"side": side, "dev": (x * ny + (y + k) % ny) * nz + z})
+        friends.append({"side": side, "dev": own_block * nz + (z + k) % nz})
+    for friend in friends:
+        pl.semaphore_signal(barrier, inc=1, device_id=friend, device_id_type=MESH)
 
     def attend(r):
         pltpu.make_async_copy(cache_ref.at[r], cache_v.at[r], cache_sem.at[r]).wait()
@@ -181,7 +182,7 @@
     for r in range(quarter):
         attend(r)
 
-    pl.semaphore_wait(barrier, side_n * ndev - 1)
+    pl.semaphore_wait(barrier, len(friends))
     for k in range(1, nx):
         remote(
             vu_ref.at[0, my_rows, :],
@@ -190,11 +191,31 @@
             vu1_sem.at[k - 1],
             at_plane(block_of(up, (uq + k) % ny)),
         ).start()
-    for k in range(1, nz):
-        to = (z + k) % nz
-        for i in range(half):
-            j = side * half + i
-            remote(wo_source(j, to), wo_place(z, j), wo_send_sem, wo_recv_sem.at[k - 1], at_ring(to)).start()
+    part_n = 2
+    step = half // part_n
+    part_lanes = step * LANES
+
+    def lanes_of(part):
+        return pl.ds(pl.multiple_of(side * half_lanes + part * part_lanes, part_lanes), part_lanes)
+
+    def exchange_wo(part):
+        for k in range(1, nz):
+            to = (z + k) % nz
+            for i in range(part * step, (part + 1) * step):
+                j = side * half + i
+                remote(
+                    wo_source(j, to), wo_place(z, j), wo_send_sem, wo_recv_sem.at[k - 1, part], at_ring(to)
+                ).start()
+
+    def swap_wo(part):
+        for k in range(1, nz):
+            drain(wo_v.at[(z + nz - k) % nz, pl.ds(0, cols), lanes_of(part)], wo_recv_sem.at[k - 1, part])
+        piece = wo_v.at[:, :, lanes_of(part)]
+        copy = remote(piece, piece, wo_swap_send_sem.at[part], wo_swap_recv_sem.at[part], mate)
+        copy.start()
+        return copy
+
+    exchange_wo(0)
     own_vu.wait()
 
     def forward_vu(a):
@@ -229,24 +250,18 @@
     for k in range(1, nz):
         to = (z + k) % nz
         remote(ctx_send.at[to], ctx_recv.at[z], ctx_send_sem, ctx_recv_sem.at[k - 1], at_ring(to)).start()
+    exchange_wo(1)
     ctx_recv[z] = ctx_send[z]
 
     for k in range(1, nx):
         for a in range(ny):
             piece = vu_v.at[block_of((up + nx - k) % nx, (uq + ny - a) % ny), my_rows, :]
             pltpu.make_async_copy(piece, piece, vu2_sem.at[k - 1, a]).wait()
-    mate = {"side": twin, "dev": dev}
     vu_half = vu_v.at[:, my_rows, :]
-    vu_swap = remote(vu_half, vu_half, sib_send_sem.at[0], sib_recv_sem.at[0], mate)
+    vu_swap = remote(vu_half, vu_half, vu_swap_send_sem, vu_swap_recv_sem, mate)
     vu_swap.start()
-    wo_half = wo_v.at[:, :, my_half]
-    own_wo = wo_v.at[z, pl.ds(0, cols), my_half]
-    pltpu.make_async_copy(own_wo, own_wo, wo_sem).wait()
-    for k in range(1, nz):
-        piece = wo_v.at[(z + nz - k) % nz, pl.ds(0, cols), my_half]
-        pltpu.make_async_copy(piece, piece, wo_recv_sem.at[k - 1]).wait()
-    wo_swap = remote(wo_half, wo_half, sib_send_sem.at[1], sib_recv_sem.at[1], mate)
-    wo_swap.start()
+    drain(wo_v.at[z, pl.ds(0, cols), my_half], wo_sem)
+    wo_swaps = [swap_wo(0)]
 
     ids = ids_ref[...]
     rw = rw_ref[...]
@@ -304,23 +319,63 @@
         ]
         val_v[my_block, jp * 2 * vdim : (jp + 1) * 2 * vdim] = jnp.concatenate(picked, axis=0).astype(BF16)
 
-    mine = val_v.at[my_block, :]
-    for k in range(1, ny):
-        remote(mine, mine, ag_send_sem, ag1_sem.at[k - 1], at_plane(block_of(up, (uq + k) % ny))).start()
-    for a in range(ny):
-        piece = val_v.at[rows_at(block_of(up, (uq + ny - a) % ny) * blk, blk), :]
-        if a > 0:
-            pltpu.make_async_copy(piece, piece, ag1_sem.at[a - 1]).wait()
-        for k in range(1, nx):
-            to = at_plane(block_of((up + k) % nx, uq))
-            remote(piece, piece, ag_send_sem, ag2_sem.at[k - 1, a], to).start()
-    wo_swap.wait_recv()
+    half_blk = blk // 2
+
+    def block_rows(w, u, part=None):
+        start = block_of(w, u) * blk
+        if part is None:
+            return val_v.at[rows_at(start, blk), :]
+        return val_v.at[rows_at(start + part * half_blk, half_blk), :]
+
+    ahead, behind = (up + 1) % nx, (up + nx - 1) % nx
+    across = (up + 2) % nx
+    u_ahead, u_behind, u_across = (uq + 1) % ny, (uq + ny - 1) % ny, (uq + 2) % ny
+
+    def pass_u(piece, forward, sem):
+        to = at_plane(block_of(up, u_ahead if forward else u_behind))
+        remote(piece, piece, ag_send_sem, ag1_sem.at[sem], to).start()
+
+    def pass_w(piece, forward, sem, a):
+        to = at_plane(block_of(ahead if forward else behind, uq))
+        remote(piece, piece, ag_send_sem, ag2_sem.at[sem, a], to).start()
+
+    mine = block_rows(up, uq)
+    pass_u(mine, True, 0)
+    pass_u(mine, False, 1)
+    pass_w(mine, True, 0, 0)
+    pass_w(mine, False, 1, 0)
+    us = [uq, u_behind, u_ahead, u_across]
+    drain(block_rows(up, u_behind), ag1_sem.at[0])
+    pass_u(block_rows(up, u_behind, 0), True, 2)
+    drain(block_rows(up, u_ahead), ag1_sem.at[1])
+    pass_u(block_rows(up, u_ahead, 1), False, 3)
+    for a in (1, 2):
+        pass_w(block_rows(up, us[a]), True, 0, a)
+        pass_w(block_rows(up, us[a]), False, 1, a)
+    drain(block_rows(up, u_across, 0), ag1_sem.at[2])
+    drain(block_rows(up, u_across, 1), ag1_sem.at[3])
+    pass_w(block_rows(up, u_across), True, 0, 3)
+    pass_w(block_rows(up, u_across), False, 1, 3)
+
+    def hand_on(a):
+        drain(block_rows(behind, us[a]), ag2_sem.at[0, a])
+        pass_w(block_rows(behind, us[a], 0), True, 2, a)
+        drain(block_rows(ahead, us[a]), ag2_sem.at[1, a])
+        pass_w(block_rows(ahead, us[a], 1), False, 3, a)
+
+    hand_on(0)
+    wo_swaps.append(swap_wo(1))
+    for swap in wo_swaps:
+        swap.wait_recv()
     for k in range(nx):
-        w = (up + nx - k) % nx
-        if k > 0:
+        w = (up, behind, ahead, across)[k]
+        if k == 1:
+            for a in range(1, ny):
+                hand_on(a)
+        if k == 3:
             for a in range(ny):
-                piece = val_v.at[rows_at(block_of(w, (uq + ny - a) % ny) * blk, blk), :]
-                pltpu.make_async_copy(piece, piece, ag2_sem.at[k - 1, a]).wait()
+                drain(block_rows(across, us[a], 0), ag2_sem.at[2, a])
+                drain(block_rows(across, us[a], 1), ag2_sem.at[3, a])
         lhs = jnp.concatenate([val_v[rows_at(block_of(w, u) * blk, blk), :] for u in range(ny)], axis=0)
         at = rows_at(w * chunk, chunk)
         own = jnp.zeros((chunk, LANES), F32)
@@ -335,7 +390,7 @@
                 part_send.at[to, at, :], part_recv.at[z, at, :], rs_send_sem, rs_recv_sem.at[kk - 1, k], at_ring(to)
             ).start()
     for k in range(nx):
-        at = rows_at(((up + nx - k) % nx) * chunk, chunk)
+        at = rows_at((up, behind, ahead, across)[k] * chunk, chunk)
         for kk in range(1, nz):
             piece = part_recv.at[(z + nz - kk) % nz, at, :]
             pltpu.make_async_copy(piece, piece, rs_recv_sem.at[kk - 1, k]).wait()
@@ -364,13 +419,16 @@
     my_lanes = rows_at(dev * LANES, LANES)
     my_slots = rows_at(side * cap, cap)
 
+    def partner(i):
+        j = (i * 91) % (side_n * ndev)
+        ss = (side + j // ndev) % side_n
+        sx = (x + (j % ndev) // (ny * nz)) % nx
+        sy = (y + (j // nz) % ny) % ny
+        sz = (z + j % nz) % nz
+        return ss, sx, sy, sz
+
     def dispatch(i, carry):
-        ds = i // ndev
-        dd = i % ndev
-        sx = (x + dd // (ny * nz)) % nx
-        sy = (y + (dd // nz) % ny) % ny
-        sz = (z + dd % nz) % nz
-        ss = (side + ds) % side_n
+        ss, sx, sy, sz = partner(i)
         expert = ss * plane + sx * ny + sy
         src = disp.at[rows_at(expert * cap, cap), :]
         remote(
@@ -415,34 +473,33 @@
 
     per = 8
     groups = ndev // per
-    first = dev // per
     home = rows_at(own_expert * cap, cap)
 
-    def give(i, carry):
-        g = (first + i) % groups
+    def spread(g, carry):
         width = per * cols
         out = nn_dot(activated, wd_v[:, pl.ds(pl.multiple_of(g * width, LANES), width)])
         for k in range(per):
             piece = out[:, k * cols : (k + 1) * cols]
             piece = jnp.concatenate([piece, jnp.zeros((slots, LANES - cols), F32)], axis=1)
             osend[:, rows_at((g * per + k) * LANES, LANES)] = piece.astype(BF16)
-        for k in range(per):
-            for s in range(side_n):
-                target = g * per + k
-                src = osend.at[s * cap : (s + 1) * cap, rows_at(target * LANES, LANES)]
-                here = (side == s) & (dev == target)
-
-                @pl.when(here)
-                def _():
-                    pltpu.make_async_copy(src, ret.at[z, home, :], ret_recv_sem).start()
-
-                @pl.when(jnp.logical_not(here))
-                def _():
-                    remote(src, ret.at[z, home, :], ret_send_sem, ret_recv_sem, {"side": s, "dev": target}).start()
-
         return carry
 
-    lax.fori_loop(0, groups, give, 0)
+    lax.fori_loop(0, groups, spread, 0)
+    pltpu.make_async_copy(osend.at[my_slots, my_lanes], ret.at[z, home, :], ret_recv_sem).start()
+
+    def give(i, carry):
+        ss, sx, sy, sz = partner(i)
+        target = (sx * ny + sy) * nz + sz
+        remote(
+            osend.at[rows_at(ss * cap, cap), rows_at(target * LANES, LANES)],
+            ret.at[z, home, :],
+            ret_send_sem,
+            ret_recv_sem,
+            {"side": ss, "dev": target},
+        ).start()
+        return carry
+
+    lax.fori_loop(1, side_n * ndev, give, 0)
 
     drain(ret, ret_recv_sem)
     total = ret[0].astype(F32)
@@ -458,9 +515,10 @@
     drain(wo_v.at[0 : nz - 1, pl.ds(0, cols), my_half], wo_send_sem)
     drain(vu_v.at[0 : (nx - 1) * (ny + 1), my_rows, :], vu_send_sem)
     vu_swap.wait_send()
-    wo_swap.wait_send()
+    for swap in wo_swaps:
+        swap.wait_send()
     drain(ctx_send.at[0 : nz - 1], ctx_send_sem)
-    drain(val_v.at[0 : (nx - 1) * (ny + 1) * blk], ag_send_sem)
+    drain(val_v.at[0 : 3 * (ny + 1) * blk], ag_send_sem)
     drain(part_send.at[0 : nz - 1], rs_send_sem)
     flat = side_n * ndev - 1
     drain(disp_drain_ref(ret, flat, cap), disp_send_sem)
@@ -487,7 +545,7 @@
 ):
     side_n = lax.axis_size("side")
     ndev = lax.axis_size("dev")
-    nx = round(ndev ** (1 / 3))
+    nx = 4
     nz = nx
     plane = nx * nx
     tokens, cols = residual.shape
@@ -536,18 +594,20 @@
             dma((3,)),
             dma(()),
             dma(()),
-            dma((nz - 1,)),
+            dma((nz - 1, 2)),
             dma(()),
             dma(()),
             dma((nx - 1,)),
             dma((nx - 1, nx)),
+            dma(()),
+            dma(()),
             dma((2,)),
             dma((2,)),
             dma(()),
             dma((nz - 1,)),
             dma(()),
-            dma((nx - 1,)),
-            dma((nx - 1, nx)),
+            dma((4,)),
+            dma((4, nx)),
             dma(()),
             dma((nz - 1, nx)),
             dma(()),

time: 93.7 us -> 87.3 us (0.932)
  the two profiles are of different devices: /device:TPU:25 before, /device:TPU:1 now
where the time goes in v2:
time: 87.3 us; the launch traced here: 87.1 us
  Pallas kernels  85.6 us (98%)
  local copies, waits for them, and re-layouts  1.55 us (2%)
    pallas_call x1, Pallas kernels, per_device(): pl.pallas_call(functools.partial(layer_kernel, {'side': side_n, 'x': nx,...  85.6 us

profile of v2, /device:TPU:1, one launch (start us, length us, event | category | flops | bytes accessed | tf_op | source)
XLA Modules:
  0.0 87.1 jit_solution(206756263426040286)
XLA Ops:
  0.0 85.6 %shard_map.118 = bf16[112,512]{1,0:T(8,128)(2,1)} custom-call(bf16[8,64,576]{2,1,0:T(8,128)(2,1)} %q_ref.1, bf16[8,576,1024]{2,1,0:T(8,128)(2,1)} %bitcast.9, s32[8]{0:T(128)} %len_ref.1, bf16[112,512]{1,0:T(8,128)(2,1)} %bitcast.14, bf16[1,512,128]{2,1,0:T(8,128)(2,1)} %vu_ref.1, bf16[112,8192]{1,0:T(8,128)(2,1)} %bitcast.12, bf16[1,112]{1,0:T(2,128)(2,1)} %bitcast.17, ...), custom_call_target="tpu_custom_call" | custom-call | tf_op jit(solution)/shard_map/pallas_call | solution.py:563
  85.6 1.6 %copy.14 = bf16[512,112]{0,1:T(8,128)(2,1)} copy(bf16[512,112]{0,1:T(8,128)(2,1)} %bitcast.13) | data formatting | bytes 229376

commit v3 on v2

v3 whole, which is shorter than its diff:
```python
import functools

import jax
import jax.numpy as jnp
from jax import lax
from jax.experimental import pallas as pl
from jax.experimental.pallas import tpu as pltpu
from jax.sharding import PartitionSpec as P

MESH = pl.DeviceIdType.MESH
LANES = 128
SCORE_SCALE = 192.0 ** (-0.5)
NORM_EPS = 1e-06
BF16 = jnp.bfloat16
F32 = jnp.float32


def nt_dot(a, b):
    return lax.dot_general(a, b, (((1,), (1,)), ((), ())), preferred_element_type=F32)


def nn_dot(a, b):
    return jnp.dot(a, b, preferred_element_type=F32)


def layer_kernel(
    dims,
    q_hbm,
    cache_ref,
    len_hbm,
    res_hbm,
    vu_ref,
    wo_ref,
    gain_hbm,
    ids_hbm,
    rw_hbm,
    wg_ref,
    wu_ref,
    wd_ref,
    out_ref,
    q_ref,
    len_ref,
    res_ref,
    gain_ref,
    ids_ref,
    rw_ref,
    cache_v,
    wg_v,
    wu_v,
    wd_v,
    wo_v,
    vu_v,
    ctx_f,
    ctx_send,
    ctx_recv,
    val_v,
    part_send,
    part_recv,
    part_own,
    res_v,
    hid_v,
    hid_t,
    pos_v,
    wte_v,
    onehot,
    wslot,
    disp,
    rows,
    osend,
    far_recv,
    near_send,
    near_recv,
    fin,
    ret,
    cache_sem,
    q_sem,
    small_sem,
    weight_sem,
    wo_sem,
    wo_send_sem,
    wo_recv_sem,
    vu_sem,
    vu_send_sem,
    vu1_sem,
    vu2_sem,
    vu_swap_send_sem,
    vu_swap_recv_sem,
    wo_swap_send_sem,
    wo_swap_recv_sem,
    ctx_send_sem,
    ctx_recv_sem,
    ag_send_sem,
    ag1_sem,
    ag2_sem,
    rs_send_sem,
    rs_recv_sem,
    disp_send_sem,
    disp_recv_sem,
    ring_send_sem,
    ring_recv_sem,
    far_send_sem,
    far_recv_sem,
    near_send_sem,
    near_recv_sem,
    ret_send_sem,
    ret_recv_sem,
):
    side_n, nx, nz = dims["side"], dims["x"], dims["z"]
    ny = nx
    plane = nx * ny
    ndev = plane * nz
    reqs, heads, _ = q_ref.shape
    length = cache_ref.shape[2]
    latent = vu_ref.shape[1]
    vdim = vu_ref.shape[2]
    cols = res_ref.shape[0]
    tokens = res_ref.shape[1]
    blk = nz * reqs
    chunk = ny * blk
    half = plane // side_n
    experts = side_n * plane
    cap = onehot.shape[0] // experts
    full = ndev * cols
    side = lax.axis_index("side")
    dev = lax.axis_index("dev")
    x = dev // (ny * nz)
    y = (dev // nz) % ny
    z = dev % nz
    own_block = x * ny + y
    up = jnp.where(side == 0, x, y)
    uq = jnp.where(side == 0, y, x)
    twin = 1 - side

    def block_of(w, u):
        return jnp.where(side == 0, w * ny + u, u * ny + w)

    def at_plane(block):
        return {"side": side, "dev": block * nz + z}

    def at_ring(zz):
        return {"side": side, "dev": own_block * nz + zz}

    def remote(src, dst, send, recv, target):
        return pltpu.make_async_remote_copy(
            src_ref=src, dst_ref=dst, send_sem=send, recv_sem=recv, device_id=target, device_id_type=MESH
        )

    def drain(ref, sem):
        pltpu.make_async_copy(ref, ref, sem).wait()

    def rows_at(start, size):
        return pl.ds(pl.multiple_of(start, size), size)

    for zz in range(nz):
        wo_v[zz, cols:, :] = jnp.zeros((LANES - cols, plane * LANES), BF16)
    barrier = pltpu.get_barrier_semaphore()
    mate = {"side": twin, "dev": dev}
    friends = [mate]
    for k in range(1, nx):
        friends.append({"side": side, "dev": (((x + k) % nx) * ny + y) * nz + z})
        friends.append({"side": side, "dev": (x * ny + (y + k) % ny) * nz + z})
        friends.append({"side": side, "dev": own_block * nz + (z + k) % nz})
    for friend in friends:
        pl.semaphore_signal(barrier, inc=1, device_id=friend, device_id_type=MESH)

    half_lanes = half * LANES
    half_rows = latent // side_n
    my_half = pl.ds(pl.multiple_of(side * half_lanes, half_lanes), half_lanes)
    my_rows = rows_at(side * half_rows, half_rows)

    def wo_source(j, zz):
        return wo_ref.at[:, rows_at((j * nz + zz) * LANES, LANES)]

    def wo_place(zz, j):
        return wo_v.at[zz, pl.ds(0, cols), rows_at(j * LANES, LANES)]

    for i in range(half):
        j = side * half + i
        pltpu.make_async_copy(wo_source(j, z), wo_place(z, j), wo_sem).start()
    own_vu = pltpu.make_async_copy(vu_ref.at[0, my_rows, :], vu_v.at[own_block, my_rows, :], vu_sem)
    own_vu.start()
    len_copy = pltpu.make_async_copy(len_hbm, len_ref, small_sem.at[0])
    len_copy.start()
    for r in range(reqs):
        pltpu.make_async_copy(q_hbm.at[r], q_ref.at[r], q_sem.at[r]).start()
        pltpu.make_async_copy(cache_ref.at[r], cache_v.at[r], cache_sem.at[r]).start()
    small_copies = [
        pltpu.make_async_copy(source, place, small_sem.at[n + 1])
        for n, (source, place) in enumerate(
            ((res_hbm, res_ref), (gain_hbm, gain_ref), (ids_hbm, ids_ref), (rw_hbm, rw_ref))
        )
    ]
    for copy in small_copies:
        copy.start()
    weight_copies = [pltpu.make_async_copy(wd_ref, wd_v, weight_sem.at[2, 0])]
    for zz in range(nz):
        for n, (source, place) in enumerate(((wg_ref, wg_v), (wu_ref, wu_v))):
            weight_copies.append(
                pltpu.make_async_copy(source.at[:, zz], place.at[zz, :, pl.ds(0, cols), :], weight_sem.at[n, zz])
            )

    def attend(r):
        pltpu.make_async_copy(q_hbm.at[r], q_ref.at[r], q_sem.at[r]).wait()
        pltpu.make_async_copy(cache_ref.at[r], cache_v.at[r], cache_sem.at[r]).wait()
        scores = nn_dot(q_ref[r], cache_v[r]) * SCORE_SCALE
        valid = lax.broadcasted_iota(jnp.int32, scores.shape, 1) < len_ref[r]
        scores = jnp.where(valid, scores, -1e30)
        weights = jnp.exp(scores - jnp.max(scores, axis=1, keepdims=True))
        weights = (weights / jnp.sum(weights, axis=1, keepdims=True)).astype(BF16)
        context = nt_dot(weights, cache_v[r, 0:latent, :])
        for b in range(latent // LANES):
            ctx_f[b, r * heads : (r + 1) * heads, :] = context[:, b * LANES : (b + 1) * LANES]

    pl.semaphore_wait(barrier, len(friends))
    for k in range(1, nx):
        remote(
            vu_ref.at[0, my_rows, :],
            vu_v.at[own_block, my_rows, :],
            vu_send_sem,
            vu1_sem.at[k - 1],
            at_plane(block_of(up, (uq + k) % ny)),
        ).start()
    cuts = (0, 3 * half // 8, half)

    def lanes_of(part):
        start = side * half_lanes + cuts[part] * LANES
        return pl.ds(pl.multiple_of(start, LANES), (cuts[part + 1] - cuts[part]) * LANES)

    def exchange_wo(part):
        for i in range(cuts[part], cuts[part + 1]):
            for k in range(1, nz):
                to = (z + k) % nz
                j = side * half + i
                remote(
                    wo_source(j, to), wo_place(z, j), wo_send_sem, wo_recv_sem.at[k - 1, part], at_ring(to)
                ).start()

    def swap_wo(part):
        for k in range(1, nz):
            drain(wo_v.at[(z + nz - k) % nz, pl.ds(0, cols), lanes_of(part)], wo_recv_sem.at[k - 1, part])
        piece = wo_v.at[:, :, lanes_of(part)]
        copy = remote(piece, piece, wo_swap_send_sem.at[part], wo_swap_recv_sem.at[part], mate)
        copy.start()
        return copy

    exchange_wo(0)

    def forward_vu(a):
        block = block_of(up, (uq + ny - a) % ny)
        piece = vu_v.at[block, my_rows, :]
        if a > 0:
            drain(piece, vu1_sem.at[a - 1])
        for k in range(1, nx):
            to = at_plane(block_of((up + k) % nx, uq))
            source = piece if a > 0 else vu_ref.at[0, my_rows, :]
            remote(source, piece, vu_send_sem, vu2_sem.at[k - 1, a], to).start()

    forward_vu(0)
    len_copy.wait()

    pairs = reqs // 2

    def send_contexts(g):
        for r in (2 * g, 2 * g + 1):
            for zz in range(nz):
                pieces = [
                    ctx_f[b, pl.ds(r * heads + zz, plane, stride=nz), :] for b in range(latent // LANES)
                ]
                ctx_send[zz, r * plane : (r + 1) * plane, :] = jnp.concatenate(pieces, axis=1).astype(BF16)
        at = pl.ds(2 * g * plane, 2 * plane)
        for k in range(1, nz):
            to = (z + k) % nz
            remote(
                ctx_send.at[to, at, :], ctx_recv.at[z, at, :], ctx_send_sem, ctx_recv_sem.at[k - 1, g], at_ring(to)
            ).start()

    for g in range(pairs):
        attend(2 * g)
        attend(2 * g + 1)
        send_contexts(g)
        if g == 1:
            for a in range(1, ny):
                forward_vu(a)
            for copy in weight_copies:
                copy.start()
    exchange_wo(1)
    ctx_recv[z] = ctx_send[z]

    def swap_vu(k):
        w = (up + nx - k) % nx
        for a in range(ny):
            block = block_of(w, (uq + ny - a) % ny)
            piece = vu_v.at[block, my_rows, :]
            if k == 0 and a == 0:
                own_vu.wait()
            elif k > 0:
                drain(piece, vu2_sem.at[k - 1, a])
            remote(piece, piece, vu_swap_send_sem, vu_swap_recv_sem, mate).start()

    for k in (0, 1, 3, 2):
        swap_vu(k)
    drain(wo_v.at[z, pl.ds(0, cols), my_half], wo_sem)
    wo_swaps = [swap_wo(0)]

    for copy in small_copies:
        copy.wait()
    ids = ids_ref[...]
    rw = rw_ref[...]
    expert_no = lax.broadcasted_iota(jnp.int32, (experts, tokens), 0)
    chosen = jnp.zeros((experts, tokens), F32)
    wte = jnp.zeros((experts, tokens), F32)
    for k in range(ids.shape[0]):
        match = ids[k : k + 1, :] == expert_no
        chosen = jnp.where(match, 1.0, chosen)
        wte = wte + jnp.where(match, rw[k : k + 1, :], 0.0)
    before = lax.broadcasted_iota(jnp.int32, (tokens, tokens), 0) < lax.broadcasted_iota(
        jnp.int32, (tokens, tokens), 1
    )
    position = nn_dot(chosen.astype(BF16), jnp.where(before, 1.0, 0.0).astype(BF16))
    pos_v[...] = jnp.where(chosen > 0.0, position, -1.0)
    wte_v[...] = wte

    def fill(e, carry):
        slot = lax.broadcasted_iota(jnp.int32, (cap, tokens), 0).astype(F32)
        hit = pos_v[pl.ds(e, 1), :] == slot
        onehot[rows_at(e * cap, cap), :] = jnp.where(hit, 1.0, 0.0).astype(BF16)
        picked = jnp.sum(jnp.where(hit, wte_v[pl.ds(e, 1), :], 0.0), axis=1, keepdims=True)
        wslot[rows_at(e * cap, cap), :] = jnp.broadcast_to(picked, (cap, LANES))
        return carry

    res_t = jnp.concatenate(
        [res_ref[...].astype(F32), jnp.zeros((LANES - cols, tokens), F32)], axis=0
    )
    res_v[...] = res_t.T
    for zz in range(nz):
        for j in range(plane):
            wg_v[zz, j, cols:, :] = jnp.zeros((LANES - cols, wg_v.shape[3]), BF16)
            wu_v[zz, j, cols:, :] = jnp.zeros((LANES - cols, wu_v.shape[3]), BF16)
    part_recv[z] = jnp.zeros((tokens, LANES), BF16)

    drain(vu_v.at[:, rows_at(twin * half_rows, half_rows), :], vu_swap_recv_sem)
    for k in range(1, nz):
        for g in range(pairs):
            drain(ctx_recv.at[(z + nz - k) % nz, pl.ds(2 * g * plane, 2 * plane), :], ctx_recv_sem.at[k - 1, g])
    my_block = rows_at(own_block * blk, blk)
    for zz in range(nz):
        for b in range(latent // LANES):
            ctx_f[b, zz * reqs * plane : (zz + 1) * reqs * plane, :] = ctx_recv[
                zz, :, b * LANES : (b + 1) * LANES
            ].astype(F32)
    for jp in range(plane // 2):
        lhs = [
            jnp.concatenate(
                [ctx_f[b, pl.ds(j, blk, stride=plane), :] for b in range(latent // LANES)], axis=1
            )
            for j in (2 * jp, 2 * jp + 1)
        ]
        rhs = jnp.concatenate([vu_v[2 * jp], vu_v[2 * jp + 1]], axis=1)
        both = nn_dot(jnp.concatenate(lhs, axis=0).astype(BF16), rhs)
        picked = jnp.concatenate([both[0:blk, 0:vdim], both[blk : 2 * blk, vdim : 2 * vdim]], axis=1)
        val_v[my_block, jp * 2 * vdim : (jp + 1) * 2 * vdim] = picked.astype(BF16)

    half_blk = blk // 2

    def block_rows(w, u, part=None):
        start = block_of(w, u) * blk
        if part is None:
            return val_v.at[rows_at(start, blk), :]
        return val_v.at[rows_at(start + part * half_blk, half_blk), :]

    ahead, behind = (up + 1) % nx, (up + nx - 1) % nx
    across = (up + 2) % nx
    u_ahead, u_behind, u_across = (uq + 1) % ny, (uq + ny - 1) % ny, (uq + 2) % ny

    def pass_u(piece, u, sem):
        remote(piece, piece, ag_send_sem, ag1_sem.at[sem], at_plane(block_of(up, u))).start()

    def pass_w(piece, forward, sem, a):
        to = at_plane(block_of(ahead if forward else behind, uq))
        remote(piece, piece, ag_send_sem, ag2_sem.at[sem, a], to).start()

    us = [uq, u_behind, u_ahead, u_across]
    mine = block_rows(up, uq)
    pass_u(mine, u_ahead, 0)
    pass_u(mine, u_behind, 1)
    pass_u(mine, u_across, 2)
    lax.fori_loop(0, experts // 4, fill, 0)
    pass_w(mine, True, 0, 0)
    pass_w(mine, False, 1, 0)
    lax.fori_loop(experts // 4, experts // 2, fill, 0)
    for a in range(1, ny):
        piece = block_rows(up, us[a])
        drain(piece, ag1_sem.at[a - 1])
        pass_w(piece, True, 0, a)
        pass_w(piece, False, 1, a)
        if a == 2:
            wo_swaps.append(swap_wo(1))

    def hand_on(a):
        drain(block_rows(behind, us[a]), ag2_sem.at[0, a])
        pass_w(block_rows(behind, us[a], 0), True, 2, a)
        drain(block_rows(ahead, us[a]), ag2_sem.at[1, a])
        pass_w(block_rows(ahead, us[a], 1), False, 3, a)

    def project(k):
        w = (up, behind, ahead, across)[k]
        lhs = jnp.concatenate([val_v[rows_at(block_of(w, u) * blk, blk), :] for u in range(ny)], axis=0)
        at = rows_at(w * chunk, chunk)
        own = jnp.zeros((chunk, LANES), F32)
        for zz in range(nz):
            part = nt_dot(lhs, wo_v[zz])
            own = jnp.where(z == zz, part, own)
            part_send[zz, at, :] = part.astype(BF16)
        part_own[at, :] = own
        for kk in range(1, nz):
            to = (z + kk) % nz
            remote(
                part_send.at[to, at, :], part_recv.at[z, at, :], rs_send_sem, rs_recv_sem.at[kk - 1, k], at_ring(to)
            ).start()

    hand_on(0)
    for swap in wo_swaps:
        swap.wait_recv()
    project(0)
    hand_on(1)
    hand_on(2)
    hand_on(3)
    project(1)
    project(2)
    lax.fori_loop(experts // 2, experts, fill, 0)
    for a in range(ny):
        drain(block_rows(across, us[a], 0), ag2_sem.at[2, a])
        drain(block_rows(across, us[a], 1), ag2_sem.at[3, a])
    project(3)
    for k in range(nx):
        at = rows_at((up, behind, ahead, across)[k] * chunk, chunk)
        for kk in range(1, nz):
            piece = part_recv.at[(z + nz - kk) % nz, at, :]
            pltpu.make_async_copy(piece, piece, rs_recv_sem.at[kk - 1, k]).wait()
    for w in range(nx):
        for u in range(ny):
            here = (w * ny + u) * blk
            total = part_own[here : here + blk, :]
            for zz in range(nz):
                total = total + part_recv[zz, here : here + blk, :].astype(F32)
            there = rows_at(block_of(w, u) * blk, blk)
            hid_v[there, :] = total + res_v[there, :]

    hidden = hid_v[...]
    squares = jnp.sum(hidden * hidden, axis=1, keepdims=True)
    high = squares.astype(BF16).astype(F32)
    middle = (squares - high).astype(BF16).astype(F32)
    low = squares - high - middle
    lane = lax.broadcasted_iota(jnp.int32, (tokens, LANES), 1)
    gain = jnp.concatenate([gain_ref[...].astype(F32), jnp.zeros((1, LANES - cols), F32)], axis=1)
    extended = hidden * gain
    extended = jnp.where(lane == cols, high, extended)
    extended = jnp.where(lane == cols + 1, middle, extended)
    extended = jnp.where(lane == cols + 2, low, extended)
    disp[...] = nn_dot(onehot[...], extended.astype(BF16)).astype(BF16)

    my_slots = rows_at(side * cap, cap)
    my_lanes = rows_at(own_block * LANES, LANES)
    own_expert = side * plane + own_block
    home = rows_at(own_expert * cap, cap)

    def dispatch(i, carry):
        ss = (side + i) % side_n
        sy = (y + (i // side_n) % ny) % ny
        dx = i // (side_n * ny)
        target = ((x + dx) % nx) * ny + sy
        remote(
            disp.at[rows_at((ss * plane + target) * cap, cap), :],
            rows.at[z, my_slots, my_lanes],
            disp_send_sem,
            disp_recv_sem.at[dx],
            {"side": ss, "dev": target * nz + z},
        ).start()
        return carry

    pltpu.make_async_copy(disp.at[home, :], rows.at[z, my_slots, my_lanes], disp_recv_sem.at[0]).start()
    lax.fori_loop(1, experts, dispatch, 0)
    hid_t[...] = hidden.T

    z_next, z_prev, z_far = (z + 1) % nz, (z + nz - 1) % nz, (z + 2) % nz
    width = ny * LANES
    slots = side_n * cap
    units = wg_v.shape[3]

    def lanes_from(p):
        return pl.ds(pl.multiple_of(p * width, width), width)

    def piece_of(zz, dx, part=None):
        lanes = lanes_from((x + nx - dx) % nx)
        if part is None:
            return rows.at[zz, :, lanes]
        return rows.at[zz, part * cap : (part + 1) * cap, lanes]

    for dx in range(nx):
        piece = piece_of(z, dx)
        drain(piece, disp_recv_sem.at[dx])
        remote(piece, piece, ring_send_sem, ring_recv_sem.at[0, dx], at_ring(z_next)).start()
        remote(piece, piece, ring_send_sem, ring_recv_sem.at[1, dx], at_ring(z_prev)).start()
    for copy in weight_copies:
        copy.wait()
    gate = jnp.zeros((slots, units), F32)
    upward = jnp.zeros((slots, units), F32)
    marks = jnp.zeros((slots, LANES), F32)

    def take(zz, gate, upward, marks):
        lhs = rows[zz]
        gate = gate + nn_dot(lhs, wg_v[zz].reshape(plane * LANES, units))
        upward = upward + nn_dot(lhs, wu_v[zz].reshape(plane * LANES, units))
        for j in range(plane):
            marks = marks + lhs[:, j * LANES : (j + 1) * LANES].astype(F32)
        return gate, upward, marks

    gate, upward, marks = take(z, gate, upward, marks)
    for dx in range(nx):
        drain(piece_of(z_prev, dx), ring_recv_sem.at[0, dx])
        piece = piece_of(z_prev, dx, 0)
        remote(piece, piece, ring_send_sem, ring_recv_sem.at[2, dx], at_ring(z_next)).start()
        drain(piece_of(z_next, dx), ring_recv_sem.at[1, dx])
        piece = piece_of(z_next, dx, 1)
        remote(piece, piece, ring_send_sem, ring_recv_sem.at[3, dx], at_ring(z_prev)).start()
    gate, upward, marks = take(z_prev, gate, upward, marks)
    gate, upward, marks = take(z_next, gate, upward, marks)
    for dx in range(nx):
        drain(piece_of(z_far, dx, 0), ring_recv_sem.at[2, dx])
        drain(piece_of(z_far, dx, 1), ring_recv_sem.at[3, dx])
    gate, upward, marks = take(z_far, gate, upward, marks)
    mark_lane = lax.broadcasted_iota(jnp.int32, (slots, LANES), 1)
    marks = jnp.where((mark_lane >= cols) & (mark_lane < cols + 3), marks, 0.0)
    scale = lax.rsqrt(jnp.sum(marks, axis=1, keepdims=True) / full + NORM_EPS)
    gate = gate * scale
    activated = (gate / (1.0 + jnp.exp(-gate)) * (upward * scale)).astype(BF16)

    top, low_half = pl.ds(0, cap), pl.ds(cap, cap)
    group = ny * nz * cols
    for k in range(nx):
        p = (x + k) % nx
        out = nn_dot(activated, wd_v[:, pl.ds(pl.multiple_of(p * group, LANES), group)])
        for a in range(ny):
            for zz in range(nz):
                at = (a * nz + zz) * cols
                piece = jnp.concatenate([out[:, at : at + cols], jnp.zeros((slots, LANES - cols), F32)], axis=1)
                osend[zz, :, rows_at((p * ny + a) * LANES, LANES)] = piece.astype(BF16)
        lanes = lanes_from(p)
        remote(
            osend.at[z_far, top, lanes], far_recv.at[0, :, lanes], far_send_sem, far_recv_sem.at[0, k], at_ring(z_next)
        ).start()
        remote(
            osend.at[z_far, low_half, lanes], far_recv.at[1, :, lanes], far_send_sem, far_recv_sem.at[1, k], at_ring(z_prev)
        ).start()
    for k in range(nx):
        lanes = lanes_from((x + k) % nx)
        remote(
            osend.at[z_next, low_half, lanes],
            near_recv.at[0, low_half, lanes],
            near_send_sem,
            near_recv_sem.at[0, k],
            at_ring(z_next),
        ).start()
        remote(
            osend.at[z_prev, top, lanes], near_recv.at[1, top, lanes], near_send_sem, near_recv_sem.at[1, k], at_ring(z_prev)
        ).start()
    for k in range(nx):
        lanes = lanes_from((x + k) % nx)
        drain(far_recv.at[0, :, lanes], far_recv_sem.at[0, k])
        near_send[0, :, lanes] = (osend[z_next, top, lanes].astype(F32) + far_recv[0, :, lanes].astype(F32)).astype(BF16)
        remote(
            near_send.at[0, :, lanes], near_recv.at[0, top, lanes], near_send_sem, near_recv_sem.at[2, k], at_ring(z_next)
        ).start()
        drain(far_recv.at[1, :, lanes], far_recv_sem.at[1, k])
        near_send[1, :, lanes] = (
            osend[z_prev, low_half, lanes].astype(F32) + far_recv[1, :, lanes].astype(F32)
        ).astype(BF16)
        remote(
            near_send.at[1, :, lanes],
            near_recv.at[1, low_half, lanes],
            near_send_sem,
            near_recv_sem.at[3, k],
            at_ring(z_prev),
        ).start()
    for k in range(nx):
        p = (x + k) % nx
        lanes = lanes_from(p)
        drain(near_recv.at[0, low_half, lanes], near_recv_sem.at[0, k])
        drain(near_recv.at[1, top, lanes], near_recv_sem.at[1, k])
        drain(near_recv.at[0, top, lanes], near_recv_sem.at[2, k])
        drain(near_recv.at[1, low_half, lanes], near_recv_sem.at[3, k])
        summed = osend[z, :, lanes].astype(F32) + near_recv[0, :, lanes].astype(F32)
        fin[:, lanes] = (summed + near_recv[1, :, lanes].astype(F32)).astype(BF16)
        for a in range(ny):
            for ds in range(side_n):
                ss = (side + ds) % side_n
                target = p * ny + (y + a) % ny
                src = fin.at[rows_at(ss * cap, cap), rows_at(target * LANES, LANES)]
                if k == 0 and a == 0 and ds == 0:
                    pltpu.make_async_copy(src, ret.at[home, :], ret_recv_sem).start()
                else:
                    to = {"side": ss, "dev": target * nz + z}
                    remote(src, ret.at[home, :], ret_send_sem, ret_recv_sem, to).start()

    drain(ret, ret_recv_sem)
    total = (ret[...].astype(F32) * wslot[...]).T
    high = total.astype(BF16)
    low = (total - high.astype(F32)).astype(BF16)
    routed = nn_dot(jnp.concatenate([high, low], axis=0), onehot[...])
    result = hid_t[...] + routed[0:LANES] + routed[LANES : 2 * LANES]
    out_ref[...] = result[0:cols]

    drain(wo_v.at[0 : nz - 1, pl.ds(0, cols), my_half], wo_send_sem)
    drain(vu_v.at[0 : (nx - 1) * (ny + 1), my_rows, :], vu_send_sem)
    drain(vu_v.at[:, my_rows, :], vu_swap_send_sem)
    for swap in wo_swaps:
        swap.wait_send()
    drain(ctx_send.at[0 : nz - 1], ctx_send_sem)
    drain(val_v.at[0 : 3 * (ny + 1) * blk], ag_send_sem)
    drain(part_send.at[0 : nz - 1], rs_send_sem)
    drain(ret.at[0 : (experts - 1) * cap], disp_send_sem)
    drain(ret.at[0 : (experts - 1) * cap], ret_send_sem)
    drain(rows.at[0:3], ring_send_sem)
    drain(far_recv, far_send_sem)
    drain(near_recv, near_send_sem)


def per_device(
    queries,
    latent_cache,
    cache_lengths,
    residual,
    value_up,
    out_proj,
    norm_gain,
    expert_ids,
    route_weights,
    w_gate,
    w_up,
    w_down,
):
    side_n = lax.axis_size("side")
    ndev = lax.axis_size("dev")
    nx = 4
    nz = nx
    plane = nx * nx
    tokens, cols = residual.shape
    reqs, heads, width = queries.shape
    length = latent_cache.shape[1]
    latent, vdim = value_up.shape[1:]
    units = w_gate.shape[1]
    experts = side_n * plane
    cap = 32
    blk = nz * reqs
    vmem = pl.BlockSpec(memory_space=pltpu.VMEM)
    hbm = pl.BlockSpec(memory_space=pl.ANY)
    dma = pltpu.SemaphoreType.DMA
    out = pl.pallas_call(
        functools.partial(layer_kernel, {"side": side_n, "x": nx, "z": nz}),
        out_shape=jax.ShapeDtypeStruct((cols, tokens), F32),
        in_specs=[hbm] * 12,
        out_specs=vmem,
        scratch_shapes=[
            pltpu.VMEM((reqs, heads, width), BF16),
            pltpu.SMEM((reqs,), jnp.int32),
            pltpu.VMEM((cols, tokens), BF16),
            pltpu.VMEM((1, cols), BF16),
            pltpu.VMEM((expert_ids.shape[1], tokens), jnp.int32),
            pltpu.VMEM((expert_ids.shape[1], tokens), F32),
            pltpu.VMEM((reqs, width, length), BF16),
            pltpu.VMEM((nz, plane, LANES, units), BF16),
            pltpu.VMEM((nz, plane, LANES, units), BF16),
            pltpu.VMEM((units, ndev * cols), BF16),
            pltpu.VMEM((nz, LANES, plane * LANES), BF16),
            pltpu.VMEM((plane, latent, vdim), BF16),
            pltpu.VMEM((latent // LANES, reqs * heads, LANES), F32),
            pltpu.VMEM((nz, plane * reqs, latent), BF16),
            pltpu.VMEM((nz, plane * reqs, latent), BF16),
            pltpu.VMEM((tokens, plane * LANES), BF16),
            pltpu.VMEM((nz, tokens, LANES), BF16),
            pltpu.VMEM((nz, tokens, LANES), BF16),
            pltpu.VMEM((tokens, LANES), F32),
            pltpu.VMEM((tokens, LANES), F32),
            pltpu.VMEM((tokens, LANES), F32),
            pltpu.VMEM((LANES, tokens), F32),
            pltpu.VMEM((experts, tokens), F32),
            pltpu.VMEM((experts, tokens), F32),
            pltpu.VMEM((experts * cap, tokens), BF16),
            pltpu.VMEM((experts * cap, LANES), F32),
            pltpu.VMEM((experts * cap, LANES), BF16),
            pltpu.VMEM((nz, side_n * cap, plane * LANES), BF16),
            pltpu.VMEM((nz, side_n * cap, plane * LANES), BF16),
            pltpu.VMEM((2, cap, plane * LANES), BF16),
            pltpu.VMEM((2, cap, plane * LANES), BF16),
            pltpu.VMEM((2, side_n * cap, plane * LANES), BF16),
            pltpu.VMEM((side_n * cap, plane * LANES), BF16),
            pltpu.VMEM((experts * cap, LANES), BF16),
            dma((reqs,)),
            dma((reqs,)),
            dma((5,)),
            dma((3, nz)),
            dma(()),
            dma(()),
            dma((nz - 1, 2)),
            dma(()),
            dma(()),
            dma((nx - 1,)),
            dma((nx - 1, nx)),
            dma(()),
            dma(()),
            dma((2,)),
            dma((2,)),
            dma(()),
            dma((nz - 1, reqs // 2)),
            dma(()),
            dma((3,)),
            dma((4, nx)),
            dma(()),
            dma((nz - 1, nx)),
            dma(()),
            dma((nx,)),
            dma(()),
            dma((4, nx)),
            dma(()),
            dma((2, nx)),
            dma(()),
            dma((4, nx)),
            dma(()),
            dma(()),
        ],
        compiler_params=pltpu.CompilerParams(
            collective_id=0, has_side_effects=True, vmem_limit_bytes=56 * 1024 * 1024
        ),
    )(
        queries,
        latent_cache.transpose(0, 2, 1),
        cache_lengths,
        residual.T,
        value_up,
        out_proj.T,
        norm_gain.reshape(1, cols),
        expert_ids.T,
        route_weights.T,
        w_gate.reshape(plane, nz, cols, units),
        w_up.reshape(plane, nz, cols, units),
        w_down,
    )
    return out.astype(BF16).T


def solution(mesh):
    placed = (
        P(("side", "dev"), None, None),
        P(("side", "dev"), None, None),
        P(("side", "dev")),
        P("side", "dev"),
        P("dev", None, None),
        P(None, "dev"),
        P("dev"),
        P("side", None),
        P("side", None),
        P(None, ("side", "dev")),
        P(None, ("side", "dev")),
        P(("side", "dev"), None),
    )
    return jax.shard_map(
        per_device, mesh=mesh, in_specs=placed, out_specs=P("side", "dev"), check_vma=False
    )
```

time: 87.3 us -> 80.5 us (0.922)
  Pallas kernels: 85.6 us -> 78.7 us
  other arithmetic: 0 us -> 1.6 us
  local copies, waits for them, and re-layouts: 1.55 us -> 0 us
    pallas_call x1, Pallas kernels: 85.6 us -> 78.7 us  [per_device(): pl.pallas_call(functools.partial(layer_kernel, {'side': side_n, 'x': nx,...]
    transpose x0 -> x1, other arithmetic: none -> 1.6 us  [per_device(): return out.astype(BF16).T]
    unnamed x1 -> x0, local copies, waits for them, and re-layouts: 1.55 us -> none
where the time goes in v3:
time: 80.5 us; the launch traced here: 80.4 us
  Pallas kernels  78.7 us (98%)
  other arithmetic  1.6 us (2%)
    pallas_call x1, Pallas kernels, per_device(): pl.pallas_call(functools.partial(layer_kernel, {'side': side_n, 'x': nx,...  78.7 us

profile of v3, /device:TPU:1, one launch (start us, length us, event | category | flops | bytes accessed | tf_op | source)
XLA Modules:
  0.0 80.4 jit_solution(1502845064492867792)
XLA Ops:
  0.0 78.7 %shard_map.118 = f32[112,512]{1,0:T(8,128)} custom-call(bf16[8,64,576]{2,1,0:T(8,128)(2,1)} %q_hbm.1, bf16[8,576,1024]{2,1,0:T(8,128)(2,1)} %bitcast.10, s32[8]{0:T(128)} %len_hbm.1, bf16[112,512]{1,0:T(8,128)(2,1)} %bitcast.14, bf16[1,512,128]{2,1,0:T(8,128)(2,1)} %vu_ref.1, bf16[112,8192]{1,0:T(8,128)(2,1)} %bitcast.13, bf16[1,112]{1,0:T(2,128)(2,1)} %bitcast.17, ...), custom_call_target="tpu_custom_call" | custom-call | tf_op jit(solution)/shard_map/pallas_call | solution.py:658
  78.8 1.6 %convert_bitcast_fusion = bf16[512,112]{0,1:T(8,128)(2,1)} fusion(f32[112,512]{1,0:T(8,128)} %shard_map.118), kind=kLoop, calls=%fused_computation | loop fusion | flops 57344 | bytes 344064 | tf_op jit(solution)/shard_map/transpose | solution.py:748

commit v4 on v3

--- a/solution.py
+++ b/solution.py
@@ -44,6 +44,7 @@
     gain_ref,
     ids_ref,
     rw_ref,
+    out_v,
     cache_v,
     wg_v,
     wu_v,
@@ -67,11 +68,10 @@
     disp,
     rows,
     osend,
-    far_recv,
-    near_send,
     near_recv,
     fin,
     ret,
+    ret_more,
     cache_sem,
     q_sem,
     small_sem,
@@ -98,8 +98,6 @@
     disp_recv_sem,
     ring_send_sem,
     ring_recv_sem,
-    far_send_sem,
-    far_recv_sem,
     near_send_sem,
     near_recv_sem,
     ret_send_sem,
@@ -174,15 +172,13 @@
     def wo_place(zz, j):
         return wo_v.at[zz, pl.ds(0, cols), rows_at(j * LANES, LANES)]
 
-    for i in range(half):
-        j = side * half + i
-        pltpu.make_async_copy(wo_source(j, z), wo_place(z, j), wo_sem).start()
     own_vu = pltpu.make_async_copy(vu_ref.at[0, my_rows, :], vu_v.at[own_block, my_rows, :], vu_sem)
     own_vu.start()
     len_copy = pltpu.make_async_copy(len_hbm, len_ref, small_sem.at[0])
     len_copy.start()
-    for r in range(reqs):
-        pltpu.make_async_copy(q_hbm.at[r], q_ref.at[r], q_sem.at[r]).start()
+    q_copy = pltpu.make_async_copy(q_hbm, q_ref, q_sem)
+    q_copy.start()
+    for r in range(2):
         pltpu.make_async_copy(cache_ref.at[r], cache_v.at[r], cache_sem.at[r]).start()
     small_copies = [
         pltpu.make_async_copy(source, place, small_sem.at[n + 1])
@@ -190,26 +186,32 @@
             ((res_hbm, res_ref), (gain_hbm, gain_ref), (ids_hbm, ids_ref), (rw_hbm, rw_ref))
         )
     ]
-    for copy in small_copies:
-        copy.start()
-    weight_copies = [pltpu.make_async_copy(wd_ref, wd_v, weight_sem.at[2, 0])]
+    weight_copies = [pltpu.make_async_copy(wd_ref, wd_v, weight_sem.at[2])]
     for zz in range(nz):
         for n, (source, place) in enumerate(((wg_ref, wg_v), (wu_ref, wu_v))):
             weight_copies.append(
-                pltpu.make_async_copy(source.at[:, zz], place.at[zz, :, pl.ds(0, cols), :], weight_sem.at[n, zz])
+                pltpu.make_async_copy(source.at[:, zz], place.at[zz, :, pl.ds(0, cols), :], weight_sem.at[n])
             )
 
-    def attend(r):
-        pltpu.make_async_copy(q_hbm.at[r], q_ref.at[r], q_sem.at[r]).wait()
-        pltpu.make_async_copy(cache_ref.at[r], cache_v.at[r], cache_sem.at[r]).wait()
-        scores = nn_dot(q_ref[r], cache_v[r]) * SCORE_SCALE
-        valid = lax.broadcasted_iota(jnp.int32, scores.shape, 1) < len_ref[r]
-        scores = jnp.where(valid, scores, -1e30)
-        weights = jnp.exp(scores - jnp.max(scores, axis=1, keepdims=True))
-        weights = (weights / jnp.sum(weights, axis=1, keepdims=True)).astype(BF16)
-        context = nt_dot(weights, cache_v[r, 0:latent, :])
-        for b in range(latent // LANES):
-            ctx_f[b, r * heads : (r + 1) * heads, :] = context[:, b * LANES : (b + 1) * LANES]
+    place_no = lax.broadcasted_iota(jnp.int32, (1, length), 1)
+
+    def attend(first):
+        pair = (first, first + 1)
+        for r in pair:
+            pltpu.make_async_copy(cache_ref.at[r], cache_v.at[r], cache_sem.at[r]).wait()
+        if first == 0:
+            for r in range(2, reqs):
+                pltpu.make_async_copy(cache_ref.at[r], cache_v.at[r], cache_sem.at[r]).start()
+        scores = []
+        for r in pair:
+            outside = jnp.where(place_no < len_ref[r], 0.0, -1e30)
+            scores.append(nn_dot(q_ref[r], cache_v[r]) * SCORE_SCALE + outside)
+        for r, own in zip(pair, scores):
+            weights = jnp.exp(own - jnp.max(own, axis=1, keepdims=True))
+            weights = (weights * (1.0 / jnp.sum(weights, axis=1, keepdims=True))).astype(BF16)
+            context = nt_dot(weights, cache_v[r, 0:latent, :])
+            for b in range(latent // LANES):
+                ctx_f[b, r * heads : (r + 1) * heads, :] = context[:, b * LANES : (b + 1) * LANES]
 
     pl.semaphore_wait(barrier, len(friends))
     for k in range(1, nx):
@@ -220,7 +222,7 @@
             vu1_sem.at[k - 1],
             at_plane(block_of(up, (uq + k) % ny)),
         ).start()
-    cuts = (0, 3 * half // 8, half)
+    cuts = (0, half // 4, half)
 
     def lanes_of(part):
         start = side * half_lanes + cuts[part] * LANES
@@ -243,8 +245,6 @@
         copy.start()
         return copy
 
-    exchange_wo(0)
-
     def forward_vu(a):
         block = block_of(up, (uq + ny - a) % ny)
         piece = vu_v.at[block, my_rows, :]
@@ -253,10 +253,11 @@
         for k in range(1, nx):
             to = at_plane(block_of((up + k) % nx, uq))
             source = piece if a > 0 else vu_ref.at[0, my_rows, :]
-            remote(source, piece, vu_send_sem, vu2_sem.at[k - 1, a], to).start()
-
-    forward_vu(0)
+            remote(source, piece, vu_send_sem, vu2_sem.at[k - 1], to).start()
+
+    exchange_wo(0)
     len_copy.wait()
+    q_copy.wait()
 
     pairs = reqs // 2
 
@@ -271,30 +272,36 @@
         for k in range(1, nz):
             to = (z + k) % nz
             remote(
-                ctx_send.at[to, at, :], ctx_recv.at[z, at, :], ctx_send_sem, ctx_recv_sem.at[k - 1, g], at_ring(to)
+                ctx_send.at[to, at, :], ctx_recv.at[z, at, :], ctx_send_sem, ctx_recv_sem.at[k - 1], at_ring(to)
             ).start()
 
     for g in range(pairs):
         attend(2 * g)
-        attend(2 * g + 1)
         send_contexts(g)
+        if g == 0:
+            forward_vu(0)
+            for i in range(half):
+                j = side * half + i
+                pltpu.make_async_copy(wo_source(j, z), wo_place(z, j), wo_sem).start()
         if g == 1:
-            for a in range(1, ny):
-                forward_vu(a)
-            for copy in weight_copies:
+            forward_vu(1)
+            forward_vu(3)
+        if g == 2:
+            forward_vu(2)
+            for copy in small_copies + weight_copies:
                 copy.start()
     exchange_wo(1)
     ctx_recv[z] = ctx_send[z]
 
     def swap_vu(k):
         w = (up + nx - k) % nx
+        if k == 0:
+            own_vu.wait()
+        else:
+            drain(vu_v.at[0:ny, my_rows, :], vu2_sem.at[k - 1])
         for a in range(ny):
             block = block_of(w, (uq + ny - a) % ny)
             piece = vu_v.at[block, my_rows, :]
-            if k == 0 and a == 0:
-                own_vu.wait()
-            elif k > 0:
-                drain(piece, vu2_sem.at[k - 1, a])
             remote(piece, piece, vu_swap_send_sem, vu_swap_recv_sem, mate).start()
 
     for k in (0, 1, 3, 2):
@@ -338,10 +345,10 @@
             wu_v[zz, j, cols:, :] = jnp.zeros((LANES - cols, wu_v.shape[3]), BF16)
     part_recv[z] = jnp.zeros((tokens, LANES), BF16)
 
+    lax.fori_loop(experts // 4, experts // 2, fill, 0)
     drain(vu_v.at[:, rows_at(twin * half_rows, half_rows), :], vu_swap_recv_sem)
     for k in range(1, nz):
-        for g in range(pairs):
-            drain(ctx_recv.at[(z + nz - k) % nz, pl.ds(2 * g * plane, 2 * plane), :], ctx_recv_sem.at[k - 1, g])
+        drain(ctx_recv.at[(z + nz - k) % nz], ctx_recv_sem.at[k - 1])
     my_block = rows_at(own_block * blk, blk)
     for zz in range(nz):
         for b in range(latent // LANES):
@@ -387,7 +394,6 @@
     lax.fori_loop(0, experts // 4, fill, 0)
     pass_w(mine, True, 0, 0)
     pass_w(mine, False, 1, 0)
-    lax.fori_loop(experts // 4, experts // 2, fill, 0)
     for a in range(1, ny):
         piece = block_rows(up, us[a])
         drain(piece, ag1_sem.at[a - 1])
@@ -395,6 +401,9 @@
         pass_w(piece, False, 1, a)
         if a == 2:
             wo_swaps.append(swap_wo(1))
+        if a == 3:
+            to = at_plane(block_of(across, uq))
+            remote(piece, piece, ag_send_sem, ag2_sem.at[2, a], to).start()
 
     def hand_on(a):
         drain(block_rows(behind, us[a]), ag2_sem.at[0, a])
@@ -415,28 +424,28 @@
         for kk in range(1, nz):
             to = (z + kk) % nz
             remote(
-                part_send.at[to, at, :], part_recv.at[z, at, :], rs_send_sem, rs_recv_sem.at[kk - 1, k], at_ring(to)
+                part_send.at[to, at, :], part_recv.at[z, at, :], rs_send_sem, rs_recv_sem.at[kk - 1], at_ring(to)
             ).start()
 
     hand_on(0)
     for swap in wo_swaps:
         swap.wait_recv()
     project(0)
+    lax.fori_loop(experts // 2, 3 * experts // 4, fill, 0)
     hand_on(1)
     hand_on(2)
-    hand_on(3)
+    for sem, w in ((0, behind), (1, ahead)):
+        drain(block_rows(w, us[3]), ag2_sem.at[sem, 3])
     project(1)
     project(2)
-    lax.fori_loop(experts // 2, experts, fill, 0)
-    for a in range(ny):
+    lax.fori_loop(3 * experts // 4, experts, fill, 0)
+    for a in range(ny - 1):
         drain(block_rows(across, us[a], 0), ag2_sem.at[2, a])
         drain(block_rows(across, us[a], 1), ag2_sem.at[3, a])
+    drain(block_rows(across, us[3]), ag2_sem.at[2, 3])
     project(3)
-    for k in range(nx):
-        at = rows_at((up, behind, ahead, across)[k] * chunk, chunk)
-        for kk in range(1, nz):
-            piece = part_recv.at[(z + nz - kk) % nz, at, :]
-            pltpu.make_async_copy(piece, piece, rs_recv_sem.at[kk - 1, k]).wait()
+    for kk in range(1, nz):
+        drain(part_recv.at[(z + nz - kk) % nz], rs_recv_sem.at[kk - 1])
     for w in range(nx):
         for u in range(ny):
             here = (w * ny + u) * blk
@@ -457,32 +466,46 @@
     extended = jnp.where(lane == cols, high, extended)
     extended = jnp.where(lane == cols + 1, middle, extended)
     extended = jnp.where(lane == cols + 2, low, extended)
-    disp[...] = nn_dot(onehot[...], extended.astype(BF16)).astype(BF16)
-
-    my_slots = rows_at(side * cap, cap)
+    part = cap // 2
+    disp[...] = nn_dot(onehot[...], extended.astype(BF16)).astype(BF16).reshape(experts, 2, part, LANES)
+
+    my_slots = rows_at(side * part, part)
     my_lanes = rows_at(own_block * LANES, LANES)
     own_expert = side * plane + own_block
-    home = rows_at(own_expert * cap, cap)
+    z_next, z_prev, z_far = (z + 1) % nz, (z + nz - 1) % nz, (z + 2) % nz
+
+    def dispatch_halves(expert, ss, target, dx):
+        for h, to in ((0, z_next), (1, z_prev)):
+            remote(
+                disp.at[expert, h],
+                rows.at[z, h, my_slots, my_lanes],
+                disp_send_sem.at[1],
+                disp_recv_sem.at[1 + h, dx],
+                {"side": ss, "dev": target * nz + to},
+            ).start()
 
     def dispatch(i, carry):
         ss = (side + i) % side_n
         sy = (y + (i // side_n) % ny) % ny
-        dx = i // (side_n * ny)
+        turn = i // (side_n * ny)
+        dx = jnp.where(turn == 0, 0, jnp.where(turn == 1, 2, jnp.where(turn == 2, 1, 3)))
         target = ((x + dx) % nx) * ny + sy
+        expert = ss * plane + target
         remote(
-            disp.at[rows_at((ss * plane + target) * cap, cap), :],
-            rows.at[z, my_slots, my_lanes],
-            disp_send_sem,
-            disp_recv_sem.at[dx],
+            disp.at[expert],
+            rows.at[z, :, my_slots, my_lanes],
+            disp_send_sem.at[0],
+            disp_recv_sem.at[0, dx],
             {"side": ss, "dev": target * nz + z},
         ).start()
+        dispatch_halves(expert, ss, target, dx)
         return carry
 
-    pltpu.make_async_copy(disp.at[home, :], rows.at[z, my_slots, my_lanes], disp_recv_sem.at[0]).start()
+    pltpu.make_async_copy(disp.at[own_expert], rows.at[z, :, my_slots, my_lanes], disp_recv_sem.at[0, 0]).start()
+    dispatch_halves(own_expert, side, own_block, 0)
     lax.fori_loop(1, experts, dispatch, 0)
     hid_t[...] = hidden.T
 
-    z_next, z_prev, z_far = (z + 1) % nz, (z + nz - 1) % nz, (z + 2) % nz
     width = ny * LANES
     slots = side_n * cap
     units = wg_v.shape[3]
@@ -490,25 +513,32 @@
     def lanes_from(p):
         return pl.ds(pl.multiple_of(p * width, width), width)
 
-    def piece_of(zz, dx, part=None):
+    def piece_of(zz, dx, h=None):
         lanes = lanes_from((x + nx - dx) % nx)
-        if part is None:
-            return rows.at[zz, :, lanes]
-        return rows.at[zz, part * cap : (part + 1) * cap, lanes]
-
-    for dx in range(nx):
-        piece = piece_of(z, dx)
-        drain(piece, disp_recv_sem.at[dx])
-        remote(piece, piece, ring_send_sem, ring_recv_sem.at[0, dx], at_ring(z_next)).start()
-        remote(piece, piece, ring_send_sem, ring_recv_sem.at[1, dx], at_ring(z_prev)).start()
-    for copy in weight_copies:
-        copy.wait()
+        if h is None:
+            return rows.at[zz, :, :, lanes]
+        return rows.at[zz, h, :, lanes]
+
+    def along(piece, to, n, dx):
+        remote(piece, piece, ring_send_sem, ring_recv_sem.at[n], at_ring(to)).start()
+
+    for dx in (0, 2, 1, 3):
+        drain(piece_of(z, dx), disp_recv_sem.at[0, dx])
+        along(piece_of(z, dx, 1), z_next, 0, dx)
+        along(piece_of(z, dx, 0), z_prev, 1, dx)
+        drain(piece_of(z_prev, dx, 0), disp_recv_sem.at[1, dx])
+        along(piece_of(z_prev, dx, 0), z_next, 2, dx)
+        drain(piece_of(z_next, dx, 1), disp_recv_sem.at[2, dx])
+        along(piece_of(z_next, dx, 1), z_prev, 3, dx)
+    weight_copies[0].wait()
+    drain(wg_v.at[:, :, pl.ds(0, cols), :], weight_sem.at[0])
+    drain(wu_v.at[:, :, pl.ds(0, cols), :], weight_sem.at[1])
     gate = jnp.zeros((slots, units), F32)
     upward = jnp.zeros((slots, units), F32)
     marks = jnp.zeros((slots, LANES), F32)
 
     def take(zz, gate, upward, marks):
-        lhs = rows[zz]
+        lhs = rows[zz].reshape(slots, plane * LANES)
         gate = gate + nn_dot(lhs, wg_v[zz].reshape(plane * LANES, units))
         upward = upward + nn_dot(lhs, wu_v[zz].reshape(plane * LANES, units))
         for j in range(plane):
@@ -516,18 +546,12 @@
         return gate, upward, marks
 
     gate, upward, marks = take(z, gate, upward, marks)
-    for dx in range(nx):
-        drain(piece_of(z_prev, dx), ring_recv_sem.at[0, dx])
-        piece = piece_of(z_prev, dx, 0)
-        remote(piece, piece, ring_send_sem, ring_recv_sem.at[2, dx], at_ring(z_next)).start()
-        drain(piece_of(z_next, dx), ring_recv_sem.at[1, dx])
-        piece = piece_of(z_next, dx, 1)
-        remote(piece, piece, ring_send_sem, ring_recv_sem.at[3, dx], at_ring(z_prev)).start()
+    drain(rows.at[z_prev, 1], ring_recv_sem.at[0])
     gate, upward, marks = take(z_prev, gate, upward, marks)
+    drain(rows.at[z_next, 0], ring_recv_sem.at[1])
     gate, upward, marks = take(z_next, gate, upward, marks)
-    for dx in range(nx):
-        drain(piece_of(z_far, dx, 0), ring_recv_sem.at[2, dx])
-        drain(piece_of(z_far, dx, 1), ring_recv_sem.at[3, dx])
+    drain(rows.at[z_far, 0], ring_recv_sem.at[2])
+    drain(rows.at[z_far, 1], ring_recv_sem.at[3])
     gate, upward, marks = take(z_far, gate, upward, marks)
     mark_lane = lax.broadcasted_iota(jnp.int32, (slots, LANES), 1)
     marks = jnp.where((mark_lane >= cols) & (mark_lane < cols + 3), marks, 0.0)
@@ -535,80 +559,64 @@
     gate = gate * scale
     activated = (gate / (1.0 + jnp.exp(-gate)) * (upward * scale)).astype(BF16)
 
-    top, low_half = pl.ds(0, cap), pl.ds(cap, cap)
     group = ny * nz * cols
-    for k in range(nx):
+    turns = (2, 1, 3, 0)
+    for k in turns:
         p = (x + k) % nx
         out = nn_dot(activated, wd_v[:, pl.ds(pl.multiple_of(p * group, LANES), group)])
         for a in range(ny):
             for zz in range(nz):
                 at = (a * nz + zz) * cols
                 piece = jnp.concatenate([out[:, at : at + cols], jnp.zeros((slots, LANES - cols), F32)], axis=1)
-                osend[zz, :, rows_at((p * ny + a) * LANES, LANES)] = piece.astype(BF16)
+                osend[zz, :, :, rows_at((p * ny + a) * LANES, LANES)] = piece.astype(BF16).reshape(
+                    2, slots // 2, LANES
+                )
         lanes = lanes_from(p)
-        remote(
-            osend.at[z_far, top, lanes], far_recv.at[0, :, lanes], far_send_sem, far_recv_sem.at[0, k], at_ring(z_next)
-        ).start()
-        remote(
-            osend.at[z_far, low_half, lanes], far_recv.at[1, :, lanes], far_send_sem, far_recv_sem.at[1, k], at_ring(z_prev)
-        ).start()
-    for k in range(nx):
-        lanes = lanes_from((x + k) % nx)
-        remote(
-            osend.at[z_next, low_half, lanes],
-            near_recv.at[0, low_half, lanes],
-            near_send_sem,
-            near_recv_sem.at[0, k],
-            at_ring(z_next),
-        ).start()
-        remote(
-            osend.at[z_prev, top, lanes], near_recv.at[1, top, lanes], near_send_sem, near_recv_sem.at[1, k], at_ring(z_prev)
-        ).start()
-    for k in range(nx):
-        lanes = lanes_from((x + k) % nx)
-        drain(far_recv.at[0, :, lanes], far_recv_sem.at[0, k])
-        near_send[0, :, lanes] = (osend[z_next, top, lanes].astype(F32) + far_recv[0, :, lanes].astype(F32)).astype(BF16)
-        remote(
-            near_send.at[0, :, lanes], near_recv.at[0, top, lanes], near_send_sem, near_recv_sem.at[2, k], at_ring(z_next)
-        ).start()
-        drain(far_recv.at[1, :, lanes], far_recv_sem.at[1, k])
-        near_send[1, :, lanes] = (
-            osend[z_prev, low_half, lanes].astype(F32) + far_recv[1, :, lanes].astype(F32)
-        ).astype(BF16)
-        remote(
-            near_send.at[1, :, lanes],
-            near_recv.at[1, low_half, lanes],
-            near_send_sem,
-            near_recv_sem.at[3, k],
-            at_ring(z_prev),
-        ).start()
-    for k in range(nx):
+        for n, (source, h, to) in enumerate(
+            ((z_next, 0, z_next), (z_prev, 1, z_prev), (z_far, 0, z_prev), (z_far, 1, z_next))
+        ):
+            remote(
+                osend.at[source, h, :, lanes], near_recv.at[n, :, lanes], near_send_sem, near_recv_sem.at[n, k], at_ring(to)
+            ).start()
+    for k in turns:
         p = (x + k) % nx
         lanes = lanes_from(p)
-        drain(near_recv.at[0, low_half, lanes], near_recv_sem.at[0, k])
-        drain(near_recv.at[1, top, lanes], near_recv_sem.at[1, k])
-        drain(near_recv.at[0, top, lanes], near_recv_sem.at[2, k])
-        drain(near_recv.at[1, low_half, lanes], near_recv_sem.at[3, k])
-        summed = osend[z, :, lanes].astype(F32) + near_recv[0, :, lanes].astype(F32)
-        fin[:, lanes] = (summed + near_recv[1, :, lanes].astype(F32)).astype(BF16)
+        for n, (held, h, place) in enumerate(((z, 0, 0), (z, 1, 1), (z_prev, 0, 2), (z_next, 1, 3))):
+            drain(near_recv.at[n, :, lanes], near_recv_sem.at[n, k])
+            summed = osend[held, h, :, lanes].astype(F32) + near_recv[n, :, lanes].astype(F32)
+            fin[place, :, lanes] = summed.astype(BF16)
         for a in range(ny):
+            target = p * ny + (y + a) % ny
+            at = rows_at(target * LANES, LANES)
             for ds in range(side_n):
                 ss = (side + ds) % side_n
-                target = p * ny + (y + a) % ny
-                src = fin.at[rows_at(ss * cap, cap), rows_at(target * LANES, LANES)]
+                its = rows_at(ss * part, part)
+                src = fin.at[0:2, its, at]
                 if k == 0 and a == 0 and ds == 0:
-                    pltpu.make_async_copy(src, ret.at[home, :], ret_recv_sem).start()
+                    pltpu.make_async_copy(src, ret.at[own_expert], ret_recv_sem.at[0]).start()
                 else:
                     to = {"side": ss, "dev": target * nz + z}
-                    remote(src, ret.at[home, :], ret_send_sem, ret_recv_sem, to).start()
-
-    drain(ret, ret_recv_sem)
-    total = (ret[...].astype(F32) * wslot[...]).T
+                    remote(src, ret.at[own_expert], ret_send_sem.at[0], ret_recv_sem.at[0], to).start()
+                for h, zz in ((0, z_prev), (1, z_next)):
+                    remote(
+                        fin.at[2 + h, its, at],
+                        ret_more.at[own_expert, h],
+                        ret_send_sem.at[1],
+                        ret_recv_sem.at[1],
+                        {"side": ss, "dev": target * nz + zz},
+                    ).start()
+
+    drain(ret, ret_recv_sem.at[0])
+    drain(ret_more, ret_recv_sem.at[1])
+    total = (ret[...].astype(F32) + ret_more[...].astype(F32)).reshape(experts * cap, LANES)
+    total = (total * wslot[...]).T
     high = total.astype(BF16)
     low = (total - high.astype(F32)).astype(BF16)
     routed = nn_dot(jnp.concatenate([high, low], axis=0), onehot[...])
     result = hid_t[...] + routed[0:LANES] + routed[LANES : 2 * LANES]
-    out_ref[...] = result[0:cols]
+    out_v[...] = result[0:cols]
+    out_copy = pltpu.make_async_copy(out_v, out_ref, small_sem.at[5])
+    out_copy.start()
 
     drain(wo_v.at[0 : nz - 1, pl.ds(0, cols), my_half], wo_send_sem)
     drain(vu_v.at[0 : (nx - 1) * (ny + 1), my_rows, :], vu_send_sem)
@@ -618,11 +626,13 @@
     drain(ctx_send.at[0 : nz - 1], ctx_send_sem)
     drain(val_v.at[0 : 3 * (ny + 1) * blk], ag_send_sem)
     drain(part_send.at[0 : nz - 1], rs_send_sem)
-    drain(ret.at[0 : (experts - 1) * cap], disp_send_sem)
-    drain(ret.at[0 : (experts - 1) * cap], ret_send_sem)
-    drain(rows.at[0:3], ring_send_sem)
-    drain(far_recv, far_send_sem)
+    drain(disp.at[0 : experts - 1], disp_send_sem.at[0])
+    drain(disp, disp_send_sem.at[1])
+    drain(ret.at[0 : experts - 1], ret_send_sem.at[0])
+    drain(ret_more, ret_send_sem.at[1])
+    drain(rows.at[0:2], ring_send_sem)
     drain(near_recv, near_send_sem)
+    out_copy.wait()
 
 
 def per_device(
@@ -652,14 +662,13 @@
     experts = side_n * plane
     cap = 32
     blk = nz * reqs
-    vmem = pl.BlockSpec(memory_space=pltpu.VMEM)
     hbm = pl.BlockSpec(memory_space=pl.ANY)
     dma = pltpu.SemaphoreType.DMA
     out = pl.pallas_call(
         functools.partial(layer_kernel, {"side": side_n, "x": nx, "z": nz}),
         out_shape=jax.ShapeDtypeStruct((cols, tokens), F32),
         in_specs=[hbm] * 12,
-        out_specs=vmem,
+        out_specs=hbm,
         scratch_shapes=[
             pltpu.VMEM((reqs, heads, width), BF16),
             pltpu.SMEM((reqs,), jnp.int32),
@@ -667,6 +676,7 @@
             pltpu.VMEM((1, cols), BF16),
             pltpu.VMEM((expert_ids.shape[1], tokens), jnp.int32),
             pltpu.VMEM((expert_ids.shape[1], tokens), F32),
+            pltpu.VMEM((cols, tokens), F32),
             pltpu.VMEM((reqs, width, length), BF16),
             pltpu.VMEM((nz, plane, LANES, units), BF16),
             pltpu.VMEM((nz, plane, LANES, units), BF16),
@@ -687,46 +697,45 @@
             pltpu.VMEM((experts, tokens), F32),
             pltpu.VMEM((experts * cap, tokens), BF16),
             pltpu.VMEM((experts * cap, LANES), F32),
-            pltpu.VMEM((experts * cap, LANES), BF16),
-            pltpu.VMEM((nz, side_n * cap, plane * LANES), BF16),
-            pltpu.VMEM((nz, side_n * cap, plane * LANES), BF16),
-            pltpu.VMEM((2, cap, plane * LANES), BF16),
-            pltpu.VMEM((2, cap, plane * LANES), BF16),
-            pltpu.VMEM((2, side_n * cap, plane * LANES), BF16),
-            pltpu.VMEM((side_n * cap, plane * LANES), BF16),
-            pltpu.VMEM((experts * cap, LANES), BF16),
+            pltpu.VMEM((experts, 2, cap // 2, LANES), BF16),
+            pltpu.VMEM((nz, 2, side_n * cap // 2, plane * LANES), BF16),
+            pltpu.VMEM((nz, 2, side_n * cap // 2, plane * LANES), BF16),
+            pltpu.VMEM((4, side_n * cap // 2, plane * LANES), BF16),
+            pltpu.VMEM((4, side_n * cap // 2, plane * LANES), BF16),
+            pltpu.VMEM((experts, 2, cap // 2, LANES), BF16),
+            pltpu.VMEM((experts, 2, cap // 2, LANES), BF16),
+        ]
+        + [
             dma((reqs,)),
-            dma((reqs,)),
-            dma((5,)),
-            dma((3, nz)),
+            dma(()),
+            dma((6,)),
+            dma((3,)),
             dma(()),
             dma(()),
             dma((nz - 1, 2)),
             dma(()),
             dma(()),
             dma((nx - 1,)),
-            dma((nx - 1, nx)),
+            dma((nx - 1,)),
             dma(()),
             dma(()),
             dma((2,)),
             dma((2,)),
             dma(()),
-            dma((nz - 1, reqs // 2)),
+            dma((nz - 1,)),
             dma(()),
             dma((3,)),
             dma((4, nx)),
             dma(()),
-            dma((nz - 1, nx)),
-            dma(()),
-            dma((nx,)),
+            dma((nz - 1,)),
+            dma((2,)),
+            dma((3, nx)),
+            dma(()),
+            dma((4,)),
             dma(()),
             dma((4, nx)),
-            dma(()),
-            dma((2, nx)),
-            dma(()),
-            dma((4, nx)),
-            dma(()),
-            dma(()),
+            dma((2,)),
+            dma((2,)),
         ],
         compiler_params=pltpu.CompilerParams(
             collective_id=0, has_side_effects=True, vmem_limit_bytes=56 * 1024 * 1024

time: 80.5 us -> 77.6 us (0.964)
  Pallas kernels: 78.7 us -> 75.8 us
    pallas_call x1, Pallas kernels: 78.7 us -> 75.8 us  [per_device(): pl.pallas_call(functools.partial(layer_kernel, {'side': side_n, 'x': nx,...]
where the time goes in v4:
time: 77.6 us; the launch traced here: 77.4 us
  Pallas kernels  75.8 us (98%)
  other arithmetic  1.6 us (2%)
    pallas_call x1, Pallas kernels, per_device(): pl.pallas_call(functools.partial(layer_kernel, {'side': side_n, 'x': nx,...  75.8 us
    transpose x1, other arithmetic, per_device(): return out.astype(BF16).T  1.6 us

profile of v4, /device:TPU:1, one launch (start us, length us, event | category | flops | bytes accessed | tf_op | source)
XLA Modules:
  0.0 77.4 jit_solution(11276475666772172298)
XLA Ops:
  0.0 75.8 %shard_map.118 = f32[112,512]{1,0:T(8,128)} custom-call(bf16[8,64,576]{2,1,0:T(8,128)(2,1)} %q_hbm.1, bf16[8,576,1024]{2,1,0:T(8,128)(2,1)} %bitcast.10, s32[8]{0:T(128)} %len_hbm.1, bf16[112,512]{1,0:T(8,128)(2,1)} %bitcast.14, bf16[1,512,128]{2,1,0:T(8,128)(2,1)} %vu_ref.1, bf16[112,8192]{1,0:T(8,128)(2,1)} %bitcast.13, bf16[1,112]{1,0:T(2,128)(2,1)} %bitcast.17, ...), custom_call_target="tpu_custom_call" | custom-call | tf_op jit(solution)/shard_map/pallas_call | solution.py:667
  75.8 1.6 %convert_bitcast_fusion = bf16[512,112]{0,1:T(8,128)(2,1)} fusion(f32[112,512]{1,0:T(8,128)} %shard_map.118), kind=kLoop, calls=%fused_computation | loop fusion | flops 57344 | bytes 344064 | tf_op jit(solution)/shard_map/transpose | solution.py:757

commit v5 on v4

--- a/solution.py
+++ b/solution.py
@@ -214,7 +214,7 @@
                 ctx_f[b, r * heads : (r + 1) * heads, :] = context[:, b * LANES : (b + 1) * LANES]
 
     pl.semaphore_wait(barrier, len(friends))
-    for k in range(1, nx):
+    for k in (1, 3, 2):
         remote(
             vu_ref.at[0, my_rows, :],
             vu_v.at[own_block, my_rows, :],
@@ -250,7 +250,7 @@
         piece = vu_v.at[block, my_rows, :]
         if a > 0:
             drain(piece, vu1_sem.at[a - 1])
-        for k in range(1, nx):
+        for k in (1, 3, 2):
             to = at_plane(block_of((up + k) % nx, uq))
             source = piece if a > 0 else vu_ref.at[0, my_rows, :]
             remote(source, piece, vu_send_sem, vu2_sem.at[k - 1], to).start()
@@ -269,7 +269,7 @@
                 ]
                 ctx_send[zz, r * plane : (r + 1) * plane, :] = jnp.concatenate(pieces, axis=1).astype(BF16)
         at = pl.ds(2 * g * plane, 2 * plane)
-        for k in range(1, nz):
+        for k in (2, 1, 3):
             to = (z + k) % nz
             remote(
                 ctx_send.at[to, at, :], ctx_recv.at[z, at, :], ctx_send_sem, ctx_recv_sem.at[k - 1], at_ring(to)
@@ -345,7 +345,7 @@
             wu_v[zz, j, cols:, :] = jnp.zeros((LANES - cols, wu_v.shape[3]), BF16)
     part_recv[z] = jnp.zeros((tokens, LANES), BF16)
 
-    lax.fori_loop(experts // 4, experts // 2, fill, 0)
+    lax.fori_loop(0, experts // 4, fill, 0)
     drain(vu_v.at[:, rows_at(twin * half_rows, half_rows), :], vu_swap_recv_sem)
     for k in range(1, nz):
         drain(ctx_recv.at[(z + nz - k) % nz], ctx_recv_sem.at[k - 1])
@@ -390,8 +390,9 @@
     mine = block_rows(up, uq)
     pass_u(mine, u_ahead, 0)
     pass_u(mine, u_behind, 1)
+    lax.fori_loop(experts // 4, experts // 2, fill, 0)
     pass_u(mine, u_across, 2)
-    lax.fori_loop(0, experts // 4, fill, 0)
+    lax.fori_loop(experts // 2, experts, fill, 0)
     pass_w(mine, True, 0, 0)
     pass_w(mine, False, 1, 0)
     for a in range(1, ny):
@@ -421,7 +422,7 @@
             own = jnp.where(z == zz, part, own)
             part_send[zz, at, :] = part.astype(BF16)
         part_own[at, :] = own
-        for kk in range(1, nz):
+        for kk in (2, 1, 3):
             to = (z + kk) % nz
             remote(
                 part_send.at[to, at, :], part_recv.at[z, at, :], rs_send_sem, rs_recv_sem.at[kk - 1], at_ring(to)
@@ -431,14 +432,12 @@
     for swap in wo_swaps:
         swap.wait_recv()
     project(0)
-    lax.fori_loop(experts // 2, 3 * experts // 4, fill, 0)
     hand_on(1)
     hand_on(2)
     for sem, w in ((0, behind), (1, ahead)):
         drain(block_rows(w, us[3]), ag2_sem.at[sem, 3])
     project(1)
     project(2)
-    lax.fori_loop(3 * experts // 4, experts, fill, 0)
     for a in range(ny - 1):
         drain(block_rows(across, us[a], 0), ag2_sem.at[2, a])
         drain(block_rows(across, us[a], 1), ag2_sem.at[3, a])
@@ -484,13 +483,16 @@
                 {"side": ss, "dev": target * nz + to},
             ).start()
 
+    def far_first(n):
+        return jnp.where(n == 1, 2, jnp.where(n == 2, 1, n))
+
     def dispatch(i, carry):
         ss = (side + i) % side_n
-        sy = (y + (i // side_n) % ny) % ny
-        turn = i // (side_n * ny)
-        dx = jnp.where(turn == 0, 0, jnp.where(turn == 1, 2, jnp.where(turn == 2, 1, 3)))
+        sy = (y + far_first((i // side_n) % ny)) % ny
+        dx = far_first(i // (side_n * ny))
         target = ((x + dx) % nx) * ny + sy
         expert = ss * plane + target
+        dispatch_halves(expert, ss, target, dx)
         remote(
             disp.at[expert],
             rows.at[z, :, my_slots, my_lanes],
@@ -498,7 +500,6 @@
             disp_recv_sem.at[0, dx],
             {"side": ss, "dev": target * nz + z},
         ).start()
-        dispatch_halves(expert, ss, target, dx)
         return carry
 
     pltpu.make_async_copy(disp.at[own_expert], rows.at[z, :, my_slots, my_lanes], disp_recv_sem.at[0, 0]).start()
@@ -585,18 +586,12 @@
             drain(near_recv.at[n, :, lanes], near_recv_sem.at[n, k])
             summed = osend[held, h, :, lanes].astype(F32) + near_recv[n, :, lanes].astype(F32)
             fin[place, :, lanes] = summed.astype(BF16)
-        for a in range(ny):
+        for a in turns:
             target = p * ny + (y + a) % ny
             at = rows_at(target * LANES, LANES)
             for ds in range(side_n):
                 ss = (side + ds) % side_n
                 its = rows_at(ss * part, part)
-                src = fin.at[0:2, its, at]
-                if k == 0 and a == 0 and ds == 0:
-                    pltpu.make_async_copy(src, ret.at[own_expert], ret_recv_sem.at[0]).start()
-                else:
-                    to = {"side": ss, "dev": target * nz + z}
-                    remote(src, ret.at[own_expert], ret_send_sem.at[0], ret_recv_sem.at[0], to).start()
                 for h, zz in ((0, z_prev), (1, z_next)):
                     remote(
                         fin.at[2 + h, its, at],
@@ -605,6 +600,12 @@
                         ret_recv_sem.at[1],
                         {"side": ss, "dev": target * nz + zz},
                     ).start()
+                src = fin.at[0:2, its, at]
+                if k == 0 and a == 0 and ds == 0:
+                    pltpu.make_async_copy(src, ret.at[own_expert], ret_recv_sem.at[0]).start()
+                else:
+                    to = {"side": ss, "dev": target * nz + z}
+                    remote(src, ret.at[own_expert], ret_send_sem.at[0], ret_recv_sem.at[0], to).start()
 
     drain(ret, ret_recv_sem.at[0])
     drain(ret_more, ret_recv_sem.at[1])

time: 77.6 us -> 76.6 us (0.987)
  Pallas kernels: 75.8 us -> 74.8 us
    pallas_call x1, Pallas kernels: 75.8 us -> 74.8 us  [per_device(): pl.pallas_call(functools.partial(layer_kernel, {'side': side_n, 'x': nx,...]
where the time goes in v5:
time: 76.6 us; the launch traced here: 76.5 us
  Pallas kernels  74.8 us (98%)
  other arithmetic  1.6 us (2%)
    pallas_call x1, Pallas kernels, per_device(): pl.pallas_call(functools.partial(layer_kernel, {'side': side_n, 'x': nx,...  74.8 us
    transpose x1, other arithmetic, per_device(): return out.astype(BF16).T  1.6 us

profile of v5, /device:TPU:1, one launch (start us, length us, event | category | flops | bytes accessed | tf_op | source)
XLA Modules:
  0.0 76.5 jit_solution(18029738363870148567)
XLA Ops:
  0.0 74.8 %shard_map.118 = f32[112,512]{1,0:T(8,128)} custom-call(bf16[8,64,576]{2,1,0:T(8,128)(2,1)} %q_hbm.1, bf16[8,576,1024]{2,1,0:T(8,128)(2,1)} %bitcast.10, s32[8]{0:T(128)} %len_hbm.1, bf16[112,512]{1,0:T(8,128)(2,1)} %bitcast.14, bf16[1,512,128]{2,1,0:T(8,128)(2,1)} %vu_ref.1, bf16[112,8192]{1,0:T(8,128)(2,1)} %bitcast.13, bf16[1,112]{1,0:T(2,128)(2,1)} %bitcast.17, ...), custom_call_target="tpu_custom_call" | custom-call | tf_op jit(solution)/shard_map/pallas_call | solution.py:668
  74.8 1.6 %convert_bitcast_fusion = bf16[512,112]{0,1:T(8,128)(2,1)} fusion(f32[112,512]{1,0:T(8,128)} %shard_map.118), kind=kLoop, calls=%fused_computation | loop fusion | flops 57344 | bytes 344064 | tf_op jit(solution)/shard_map/transpose | solution.py:758

commit v6 on v5

--- a/solution.py
+++ b/solution.py
@@ -466,7 +466,7 @@
     extended = jnp.where(lane == cols + 1, middle, extended)
     extended = jnp.where(lane == cols + 2, low, extended)
     part = cap // 2
-    disp[...] = nn_dot(onehot[...], extended.astype(BF16)).astype(BF16).reshape(experts, 2, part, LANES)
+    extended = extended.astype(BF16)
 
     my_slots = rows_at(side * part, part)
     my_lanes = rows_at(own_block * LANES, LANES)
@@ -502,9 +502,19 @@
         ).start()
         return carry
 
-    pltpu.make_async_copy(disp.at[own_expert], rows.at[z, :, my_slots, my_lanes], disp_recv_sem.at[0, 0]).start()
-    dispatch_halves(own_expert, side, own_block, 0)
-    lax.fori_loop(1, experts, dispatch, 0)
+    for turn in range(nx):
+        column = (x + (0, 2, 1, 3)[turn]) % nx
+        for ss in range(side_n):
+            first = ss * plane + column * ny
+            picked = nn_dot(onehot[rows_at(first * cap, ny * cap), :], extended)
+            disp[pl.ds(first, ny)] = picked.astype(BF16).reshape(ny, 2, part, LANES)
+        if turn == 0:
+            pltpu.make_async_copy(
+                disp.at[own_expert], rows.at[z, :, my_slots, my_lanes], disp_recv_sem.at[0, 0]
+            ).start()
+            dispatch_halves(own_expert, side, own_block, 0)
+        per_turn = side_n * ny
+        lax.fori_loop(max(1, turn * per_turn), (turn + 1) * per_turn, dispatch, 0)
     hid_t[...] = hidden.T
 
     width = ny * LANES

time: 76.6 us -> 75.5 us (0.986)
  Pallas kernels: 74.8 us -> 73.8 us
    pallas_call x1, Pallas kernels: 74.8 us -> 73.8 us  [per_device(): pl.pallas_call(functools.partial(layer_kernel, {'side': side_n, 'x': nx,...]
where the time goes in v6:
time: 75.5 us; the launch traced here: 75.4 us
  Pallas kernels  73.8 us (98%)
  other arithmetic  1.6 us (2%)
    pallas_call x1, Pallas kernels, per_device(): pl.pallas_call(functools.partial(layer_kernel, {'side': side_n, 'x': nx,...  73.8 us
    transpose x1, other arithmetic, per_device(): return out.astype(BF16).T  1.6 us

profile of v6, /device:TPU:1, one launch (start us, length us, event | category | flops | bytes accessed | tf_op | source)
XLA Modules:
  0.0 75.4 jit_solution(11015109392973981448)
XLA Ops:
  0.0 73.8 %shard_map.118 = f32[112,512]{1,0:T(8,128)} custom-call(bf16[8,64,576]{2,1,0:T(8,128)(2,1)} %q_hbm.1, bf16[8,576,1024]{2,1,0:T(8,128)(2,1)} %bitcast.10, s32[8]{0:T(128)} %len_hbm.1, bf16[112,512]{1,0:T(8,128)(2,1)} %bitcast.14, bf16[1,512,128]{2,1,0:T(8,128)(2,1)} %vu_ref.1, bf16[112,8192]{1,0:T(8,128)(2,1)} %bitcast.13, bf16[1,112]{1,0:T(2,128)(2,1)} %bitcast.17, ...), custom_call_target="tpu_custom_call" | custom-call | tf_op jit(solution)/shard_map/pallas_call | solution.py:678
  73.8 1.6 %convert_bitcast_fusion = bf16[512,112]{0,1:T(8,128)(2,1)} fusion(f32[112,512]{1,0:T(8,128)} %shard_map.118), kind=kLoop, calls=%fused_computation | loop fusion | flops 57344 | bytes 344064 | tf_op jit(solution)/shard_map/transpose | solution.py:768
